TPU v7x, 128 devices: a whole 4x4x4 slice. The times are simulated.
128 devices in a mesh: seq: 16 (over z, y), tp: 8 (over x, core).
Axes of the slice: x: 4, y: 4, z: 4, core: 2. Of those that a mesh axis runs over, the one named last changes fastest.
Arguments:
- normed: bfloat16 [4, 16384, 1024], P(None, 'seq'), may hold values from -6 to 6
- grad_out: bfloat16 [4, 16384, 1024], P(None, 'seq'), may hold values from -16 to 16
- value_weight: bfloat16 [1024, 1024], P(None, 'tp'), may hold values from -0.1875 to 0.1875
- gate_weight: bfloat16 [1024, 1024], P(None, 'tp'), may hold values from -0.1875 to 0.1875
- depth_taps: float32 [9, 1024], P(None, 'tp'), may hold values from -2 to 2
- norm_gain: float32 [1024], P('tp'), may hold values from 0.1 to 1.9
- norm_shift: float32 [1024], P('tp'), may hold values from -1 to 1
- out_weight: bfloat16 [1024, 1024], P(None, 'tp'), may hold values from -0.1875 to 0.1875
- lengths: int32 [4], replicated, may hold values from 4096 to 16384, as said below
Outputs:
- grad_in: bfloat16 [4, 1024, 16384], P(None, ('seq', 'tp'))
- grad_w_value: float32 [1024, 1024], P('seq', 'tp')
- grad_w_gate: float32 [1024, 1024], P('seq', 'tp')
- grad_w_out: float32 [1024, 1024], P('seq', 'tp')
- grad_taps: float32 [9, 1024], P(None, 'tp')
- grad_gain: float32 [1024], P('tp')
- grad_shift: float32 [1024], P('tp')
Inputs may be any that keep to these rules, and one draw needn't show every extreme that they name: `lengths`: frames of each recording that are valid; some recording is valid to its last frame.
All inputs are finite; a program needn't handle non-finite values.
Results may differ from a plain program's by a relative error of at most 0.01.
Values may be sent and summed in bfloat16 or wider, within the bound.
A program may use at most 128 MiB of HBM per device.

v0:
```python
import jax
import jax.numpy as jnp
from jax import lax
from jax.sharding import PartitionSpec as P

epsilon = 1e-05


def extended(block, sides, width):
    for axis, dim in sides:
        count = lax.axis_size(axis)
        forward = [(i, i + 1) for i in range(count - 1)]
        backward = [(target, source) for source, target in forward]
        low = lax.ppermute(
            lax.slice_in_dim(block, block.shape[dim] - width, None, axis=dim), axis, forward
        )
        high = lax.ppermute(lax.slice_in_dim(block, 0, width, axis=dim), axis, backward)
        block = jnp.concatenate([low, block, high], axis=dim)
    return block


def frame_edges(field, margin):
    return extended(field, (("seq", 1),), margin)


def channel_sums(parts):
    return lax.psum(parts, "seq")


def per_device(
    normed,
    grad_out,
    value_weight,
    gate_weight,
    depth_taps,
    norm_gain,
    norm_shift,
    out_weight,
    lengths,
):
    record_count, frames, model_width = normed.shape
    kernel = depth_taps.shape[0]
    margin = (kernel - 1) // 2
    local_width = value_weight.shape[1]
    seq_count = lax.axis_size("seq")
    tp_count = lax.axis_size("tp")
    piece_width = model_width // (seq_count * tp_count)
    group_place = lax.axis_index("tp")
    positions = lax.axis_index("seq") * frames + jnp.arange(frames, dtype=jnp.int32)
    valid_mask = (positions[None, :] < lengths[:, None]).astype(jnp.float32)[:, :, None]
    frame_count = jnp.sum(lengths).astype(jnp.float32)
    rows_in = normed.reshape(record_count * frames, model_width)
    value_lin = jnp.dot(rows_in, value_weight, preferred_element_type=jnp.float32).reshape(
        record_count, frames, local_width
    )
    gate_lin = jnp.dot(rows_in, gate_weight, preferred_element_type=jnp.float32).reshape(
        record_count, frames, local_width
    )
    gate_sig = jax.nn.sigmoid(gate_lin)
    gated_units = valid_mask * value_lin * gate_sig
    gated_pad = frame_edges(gated_units, margin)
    conv_out = jnp.zeros((record_count, frames, local_width), jnp.float32)
    for tap_index in range(kernel):
        conv_out = conv_out + depth_taps[tap_index] * lax.slice_in_dim(
            gated_pad, tap_index, tap_index + frames, axis=1
        )
    channel_sum, channel_sq = channel_sums(
        (
            jnp.sum(valid_mask * conv_out, axis=(0, 1)),
            jnp.sum(valid_mask * conv_out * conv_out, axis=(0, 1)),
        )
    )
    centre = channel_sum / frame_count
    spread = channel_sq / frame_count - centre * centre
    inv_std = lax.rsqrt(spread + epsilon)
    unit_conv = (conv_out - centre) * inv_std
    normalized = unit_conv * norm_gain + norm_shift
    norm_sig = jax.nn.sigmoid(normalized)
    swished = (valid_mask * normalized * norm_sig).astype(jnp.bfloat16)
    grads_flat = grad_out.reshape(record_count * frames, model_width)
    swish_grad = jnp.dot(grads_flat, out_weight, preferred_element_type=jnp.float32).reshape(
        record_count, frames, local_width
    )
    grad_w_out = lax.dot_general(
        grads_flat,
        swished.reshape(record_count * frames, local_width),
        (((0,), (0,)), ((), ())),
        preferred_element_type=jnp.float32,
    )
    grad_norm = swish_grad * valid_mask * norm_sig * (1.0 + normalized * (1.0 - norm_sig))
    shift_part = jnp.sum(grad_norm, axis=(0, 1))
    gain_part = jnp.sum(grad_norm * unit_conv, axis=(0, 1))
    grad_shift, grad_gain = channel_sums((shift_part, gain_part))
    grad_conv = (
        valid_mask
        * norm_gain
        * inv_std
        * (grad_norm - grad_shift / frame_count - unit_conv * grad_gain / frame_count)
    )
    tap_list = []
    for tap_index in range(kernel):
        window = lax.slice_in_dim(gated_pad, tap_index, tap_index + frames, axis=1)
        tap_list.append(jnp.sum(grad_conv * window, axis=(0, 1)))
    grad_taps = channel_sums(jnp.stack(tap_list))
    conv_pad = frame_edges(grad_conv, margin)
    grad_gated = jnp.zeros((record_count, frames, local_width), jnp.float32)
    for tap_index in range(kernel):
        first_row = 2 * margin - tap_index
        grad_gated = grad_gated + depth_taps[tap_index] * lax.slice_in_dim(
            conv_pad, first_row, first_row + frames, axis=1
        )
    grad_gated = valid_mask * grad_gated
    grad_value = (
        (grad_gated * gate_sig).astype(jnp.bfloat16).reshape(record_count * frames, local_width)
    )
    grad_gate = (
        (grad_gated * value_lin * gate_sig * (1.0 - gate_sig))
        .astype(jnp.bfloat16)
        .reshape(record_count * frames, local_width)
    )
    grad_w_value = lax.dot_general(
        rows_in, grad_value, (((0,), (0,)), ((), ())), preferred_element_type=jnp.float32
    )
    grad_w_gate = lax.dot_general(
        rows_in, grad_gate, (((0,), (0,)), ((), ())), preferred_element_type=jnp.float32
    )
    partial_value = lax.dot_general(
        grad_value, value_weight, (((1,), (1,)), ((), ())), preferred_element_type=jnp.float32
    )
    partial_value = partial_value + lax.dot_general(
        grad_gate, gate_weight, (((1,), (1,)), ((), ())), preferred_element_type=jnp.float32
    )
    split_partial = partial_value.reshape(record_count, frames, seq_count, tp_count, piece_width)
    channel_partial = jnp.transpose(split_partial, (0, 2, 3, 4, 1))
    summed = lax.psum_scatter(
        channel_partial.astype(jnp.bfloat16), "tp", scatter_dimension=2, tiled=True
    ).astype(jnp.float32)
    grad_normed = summed.reshape(record_count, seq_count, piece_width, frames)
    split_grads = grad_out.reshape(record_count, frames, seq_count, tp_count, piece_width)
    own_grads = lax.dynamic_slice_in_dim(split_grads, group_place, 1, 3).reshape(
        record_count, frames, seq_count, piece_width
    )
    own_major = jnp.transpose(own_grads, (0, 2, 3, 1))
    grad_slice = (own_major.astype(jnp.float32) + grad_normed).astype(jnp.bfloat16)
    moved = lax.all_to_all(grad_slice, "seq", split_axis=1, concat_axis=3, tiled=True)
    grad_in = moved.reshape(record_count, piece_width, seq_count * frames)
    grad_w_value, grad_w_gate, grad_w_out = (
        lax.psum_scatter(grad_w_value, "seq", scatter_dimension=0, tiled=True),
        lax.psum_scatter(grad_w_gate, "seq", scatter_dimension=0, tiled=True),
        lax.psum_scatter(grad_w_out, "seq", scatter_dimension=0, tiled=True),
    )
    return (grad_in, grad_w_value, grad_w_gate, grad_w_out, grad_taps, grad_gain, grad_shift)


def solution(mesh):
    placed = (
        P(None, "seq", None),
        P(None, "seq", None),
        P(None, "tp"),
        P(None, "tp"),
        P(None, "tp"),
        P("tp"),
        P("tp"),
        P(None, "tp"),
        P(),
    )
    return jax.shard_map(
        per_device,
        mesh=mesh,
        in_specs=placed,
        out_specs=(
            P(None, ("seq", "tp"), None),
            P("seq", "tp"),
            P("seq", "tp"),
            P("seq", "tp"),
            P(None, "tp"),
            P("tp"),
            P("tp"),
        ),
        check_vma=False,
    )
```

profile of v0, /device:TPU:0, one launch (start us, length us, event | category | flops | bytes accessed | tf_op | source)
XLA Modules:
  0.0 477.0 jit_solution(16447899580565461981)
XLA Ops:
  7.2 0.0 reduce-scatter.11.cloned.1.call-start
  7.3 6.0 %fusion.39 = f32[4,1024,128]{2,1,0:T(8,128)S(1)} fusion(bf16[4,1024,1024]{2,1,0:T(8,128)(2,1)} %param.9, bf16[1024,128]{1,0:T(8,128)(2,1)} %param.11), kind=kOutput, calls=%fused_computation.87 | convolution fusion | flops 1073741824 | bytes 10747904 | tf_op jit(solution)/shard_map/dot_general | solution.py:53
  13.2 0.1 compare_convert_fusion
  13.3 3.6 multiply_multiply_fusion.1
  16.9 1.3 collective-permute-start.1
  18.2 4.5 collective-permute-start
  22.8 0.6 reduce_sum.127
  24.1 0.0 collective-permute-done
  24.2 3.8 fusion
  28.0 43.0 %all-reduce.1 = (f32[128]{0:T(128)S(1)}, f32[128]{0:T(128)S(1)}) all-reduce(f32[128]{0:T(128)S(1)} %get-tuple-element.49, f32[128]{0:T(128)S(1)} %get-tuple-element.48), channel_id=1, replica_groups=mesh['seq'=16,'tp'=8] {'seq'}, use_global_device_ids=true, to_apply=%region_4.0 | all-reduce | flops 256 | bytes 2048 | tf_op jit(solution)/shard_map/psum | solution.py:27
  71.0 8.1 %fusion.42 = (f32[128]{0:T(128)S(1)}, f32[128]{0:T(128)S(1)}, f32[4,1024,128]{2,1,0:T(8,128)}) fusion(f32[128]{0:T(128)S(1)} %get-tuple-element.59, f32[4,1024,128]{2,1,0:T(8,128)} %get-tuple-element.61, f32[128]{0:T(128)S(1)} %get-tuple-element.60, f32[128]{0:T(128)S(1)} %copy-done.12, f32[128]{0:T(128)S(1)} %copy-done.8, ...), kind=kOutput, calls=%fused_computation.105 | convolution fusion | flops 1082130176 | bytes 12864512 | tf_op jit(solution)/shard_map/dot_general | solution.py:81
  79.1 35.4 %all-reduce = (f32[128]{0:T(128)S(1)}, f32[128]{0:T(128)S(1)}) all-reduce(f32[128]{0:T(128)S(1)} %get-tuple-element.51, f32[128]{0:T(128)S(1)} %get-tuple-element.50), channel_id=1, replica_groups=mesh['seq'=16,'tp'=8] {'seq'}, use_global_device_ids=true, to_apply=%region_8.0 | all-reduce | flops 256 | bytes 2048 | tf_op jit(solution)/shard_map/psum | solution.py:27
  114.5 6.6 %multiply_reduce_fusion.1 = (f32[128]{0:T(128)S(1)}, f32[128]{0:T(128)S(1)}, f32[128]{0:T(128)S(1)}, f32[128]{0:T(128)S(1)}, f32[128]{0:T(128)S(1)}, /*index=5*/...) fusion(f32[4,4,128]{2,1,0:T(4,128)S(1)} %collective-permute-done.1, ...), kind=kLoop, calls=%fused_computation.55 | loop fusion | flops 18348928 | bytes 8428548 | tf_op jit(solution)/shard_map/reduce_sum | solution.py:103
  121.2 3.9 collective-permute-start.3
  125.1 1.5 collective-permute-start.2
  126.6 4.1 collective-permute-done.2
  130.6 3.0 multiply_convert_fusion.1
  133.7 0.2 multiply_convert_fusion.2
  133.9 0.7 copy-done.6
  134.6 8.1 %fusion.46 = f32[4096,1024]{1,0:T(8,128)} fusion(bf16[4096,128]{1,0:T(8,128)(2,1)S(1)} %bitcast.94, bf16[1024,128]{1,0:T(8,128)(2,1)S(1)} %copy-done.6), kind=kOutput, calls=%fused_computation.108 | convolution fusion | flops 1073741824 | bytes 18087936 | tf_op jit(solution)/shard_map/dot_general | solution.py:127
  142.7 11.3 %add_convert_fusion = bf16[4096,1024]{1,0:T(8,128)(2,1)} fusion(f32[4096,1024]{1,0:T(8,128)} %fusion.46, bf16[4096,128]{1,0:T(8,128)(2,1)S(1)} %bitcast.95, bf16[1024,128]{1,0:T(8,128)(2,1)S(1)} %copy-done), kind=kOutput, calls=%fused_computation | convolution fusion | flops 1082130432 | bytes 26476544 | tf_op jit(solution)/shard_map/dot_general | solution.py:130
  154.0 11.3 %copy.44 = bf16[4096,1024]{0,1:T(8,128)(2,1)} copy(bf16[4096,1024]{1,0:T(8,128)(2,1)} %add_convert_fusion) | data formatting | bytes 16777216 | tf_op jit(solution)/shard_map/convert_element_type | solution.py:136
  165.3 14.6 %convert_element_type.49 = bf16[4,1024,16,8,8]{1,0,4,3,2:T(4,128)(2,1)} reshape(bf16[4096,1024]{0,1:T(8,128)(2,1)} %copy.44) | data formatting | bytes 16777216 | tf_op jit(solution)/shard_map/convert_element_type | solution.py:136
  179.8 9.8 %copy.64 = bf16[4,1024,16,8,8]{1,4,2,0,3:T(8,128)(2,1)} copy(bf16[4,1024,16,8,8]{1,0,4,3,2:T(4,128)(2,1)} %convert_element_type.49) | data formatting | bytes 16777216 | tf_op jit(solution)/shard_map/convert_element_type | solution.py:136
  189.6 0.0 reduce-scatter.11.cloned.1.call-update
  189.7 0.0 reduce-scatter.17.cloned.1.call-start
  189.7 6.4 %convolution_bitcast_fusion = f32[1024,128]{0,1:T(8,128)S(1)} fusion(bf16[4,1024,1024]{2,1,0:T(8,128)(2,1)} %param.10, f32[4,1024,128]{2,1,0:T(8,128)} %get-tuple-element.61, f32[128]{0:T(128)S(1)} %copy-done.12, f32[128]{0:T(128)S(1)} %get-tuple-element.60, f32[128]{0:T(128)S(1)} %get-tuple-element.59, f32[128]{0:T(128)S(1)} %copy-done.8, ...), kind=kOutput, calls=%fused_computation.76 | convolution fusion | flops 1078984704 | bytes 11028480 | tf_op jit(solution)/shard_map/dot_general | solution.py:84
  196.1 1.0 copy.61
  197.1 0.0 reduce-scatter.17.cloned.1.call-update
  197.1 0.3 reduce-scatter.13.cloned.1.call-start
  197.4 4.7 convolution_bitcast_fusion.2
  202.1 1.0 copy.57
  203.1 0.0 reduce-scatter.13.cloned.1.call-update
  203.1 0.0 reduce-scatter.15.cloned.1.call-start
  203.2 11.5 %copy.43 = bf16[4,1024,1024]{1,2,0:T(8,128)(2,1)} copy(bf16[4,1024,1024]{2,1,0:T(8,128)(2,1)} %param.10) | data formatting | bytes 16777216 | tf_op args[1]
  214.7 4.8 %convolution_bitcast_fusion.1 = f32[1024,128]{0,1:T(8,128)S(1)} fusion(bf16[4,1024,128]{2,1,0:T(8,128)(2,1)S(1)} %get-tuple-element.57, bf16[4,1024,1024]{2,1,0:T(8,128)(2,1)} %param.9), kind=kOutput, calls=%fused_computation.77 | convolution fusion | flops 1073741824 | bytes 9961472 | tf_op jit(solution)/shard_map/dot_general | solution.py:124
  219.5 1.0 copy.59
  220.5 0.0 reduce-scatter.15.cloned.1.call-update
  220.6 18.8 %reduce-scatter.11.cloned.1.call-done = bf16[4,16,1,8,1024]{4,3,1,0,2:T(8,128)(2,1)} async-done(((bf16[4,16,8,8,1024]{4,3,1,0,2:T(8,128)(2,1)}), bf16[4,16,1,8,1024]{4,3,1,0,2:T(8,128)(2,1)}) %reduce-scatter.11.cloned.1.call-update) | async-done | bytes 1048592 | tf_op jit(solution)/shard_map/reduce_scatter | solution.py:135
  239.4 1.9 fusion.30
  241.3 1.1 copy.46
  242.4 7.0 %all-to-all-start = ((bf16[4,16,8,1024]{3,2,0,1:T(8,128)(2,1)}), bf16[4,16,8,1024]{3,2,0,1:T(8,128)(2,1)S(1)}, u32[]{:S(2)}, u32[]{:S(2)}) async-start(bf16[4,16,8,1024]{3,2,0,1:T(8,128)(2,1)} %copy.46), calls=%async_computation.1 | async-start | bytes 2097152 | tf_op jit(solution)/shard_map/all_to_all | solution.py:145
  249.4 46.2 %psum.39 = f32[9,128]{1,0:T(8,128)} all-reduce(f32[9,128]{1,0:T(8,128)S(1)} %stack.39), channel_id=1, replica_groups=mesh['seq'=16,'tp'=8] {'seq'}, use_global_device_ids=true, to_apply=%region_22.0 | all-reduce | flops 1152 | bytes 9216 | tf_op jit(solution)/shard_map/psum | solution.py:27
  295.6 0.6 copy.47
  296.2 1.3 reshape.103
  297.5 22.0 %reduce-scatter.17.cloned.1.call-done = f32[64,128]{1,0:T(8,128)} async-done(((f32[1024,128]{1,0:T(8,128)}), f32[64,128]{1,0:T(8,128)}) %reduce-scatter.17.cloned.1.call-update) | async-done | bytes 32784
  319.5 75.7 %reduce-scatter.13.cloned.1.call-done = f32[64,128]{1,0:T(8,128)} async-done(((f32[1024,128]{1,0:T(8,128)}), f32[64,128]{1,0:T(8,128)}) %reduce-scatter.13.cloned.1.call-update) | async-done | bytes 32784
  395.2 75.3 %reduce-scatter.15.cloned.1.call-done = f32[64,128]{1,0:T(8,128)} async-done(((f32[1024,128]{1,0:T(8,128)}), f32[64,128]{1,0:T(8,128)}) %reduce-scatter.15.cloned.1.call-update) | async-done | bytes 32784
  (37 shorter events, 0.2 us)
Async XLA Ops:
  7.2 6.2 %copy-start = (bf16[1024,128]{1,0:T(8,128)(2,1)S(1)}, bf16[1024,128]{1,0:T(8,128)(2,1)}, u32[]{:S(2)}) copy-start(bf16[1024,128]{1,0:T(8,128)(2,1)} %param.12) | copy-start | bytes 786436
  7.2 232.2 %reduce-scatter.11.cloned.1.call-start = ((), (), s32[]{:S(2)}) async-start(), calls=%async_computation.5 | async-start | bytes 9437184 | tf_op jit(solution)/shard_map/reduce_scatter | solution.py:135
  7.2 6.0 %copy-start.10 = (s32[4]{0:T(128)S(1)}, s32[4]{0:T(128)}, u32[]{:S(2)}) copy-start(s32[4]{0:T(128)} %param.17) | copy-start | bytes 52
  7.3 6.1 %copy-start.2 = (bf16[4,1024,1024]{2,1,0:T(8,128)(2,1)S(1)}, bf16[4,1024,1024]{2,1,0:T(8,128)(2,1)}, u32[]{:S(2)}) copy-start(bf16[4,1024,1024]{2,1,0:T(8,128)(2,1)} %param.9) | copy-start | bytes 25165828
  13.2 3.7 copy-start.4
  13.3 9.5 %copy-start.7 = (f32[9,128]{1,0:T(8,128)S(1)}, f32[9,128]{1,0:T(8,128)}, u32[]{:S(2)}) copy-start(f32[9,128]{1,0:T(8,128)} %param.13) | copy-start | bytes 13828
  16.9 7.2 %collective-permute-start.1 = (f32[4,4,128]{2,1,0:T(4,128)S(1)}, f32[4,4,128]{2,1,0:T(4,128)S(1)}, u32[]{:S(2)}, u32[]{:S(2)}) collective-permute-start(f32[4,4,128]{2,1,0:T(4,128)S(1)} %get-tuple-element.65), channel_id=1, source_target_pairs={{8,0},{16,8},{24,16},{32,24},{40,32},{48,40},{56,48},{64,56},{72,6... | collective-permute-start | bytes 24584 | tf_op jit(solution)/shard_map/ppermute | solution.py:17
  18.2 5.9 %collective-permute-start = (f32[4,4,128]{2,1,0:T(4,128)S(1)}, f32[4,4,128]{2,1,0:T(4,128)S(1)}, u32[]{:S(2)}, u32[]{:S(2)}) collective-permute-start(f32[4,4,128]{2,1,0:T(4,128)S(1)} %get-tuple-element.64), channel_id=1, source_target_pairs={{0,8},{8,16},{16,24},{24,32},{32,40},{40,48},{48,56},{56,64},{64,7... | collective-permute-start | bytes 24584 | tf_op jit(solution)/shard_map/ppermute | solution.py:14
  24.1 46.8 %copy-start.8 = (f32[128]{0:T(128)S(1)}, f32[128]{0:T(128)}, u32[]{:S(2)}) copy-start(f32[128]{0:T(128)} %param.14) | copy-start | bytes 1540
  24.2 46.8 %copy-start.11 = (bf16[1024,128]{1,0:T(8,128)(2,1)S(1)}, bf16[1024,128]{1,0:T(8,128)(2,1)}, u32[]{:S(2)}) copy-start(bf16[1024,128]{1,0:T(8,128)(2,1)} %param.16) | copy-start | bytes 786436
  24.2 46.8 %copy-start.12 = (f32[128]{0:T(128)S(1)}, f32[128]{0:T(128)}, u32[]{:S(2)}) copy-start(f32[128]{0:T(128)} %param.15) | copy-start | bytes 1540
  114.5 6.6 %copy-start.9 = (f32[128]{0:T(128)}, f32[128]{0:T(128)S(1)}, u32[]{:S(2)}) copy-start(f32[128]{0:T(128)S(1)} %get-tuple-element.52) | copy-start | bytes 1540
  114.5 6.6 %copy-start.13 = (f32[128]{0:T(128)}, f32[128]{0:T(128)S(1)}, u32[]{:S(2)}) copy-start(f32[128]{0:T(128)S(1)} %get-tuple-element.53) | copy-start | bytes 1540
  114.5 16.1 %copy-start.3 = (f32[4,1024,128]{2,1,0:T(8,128)S(1)}, f32[4,1024,128]{2,1,0:T(8,128)}, u32[]{:S(2)}) copy-start(f32[4,1024,128]{2,1,0:T(8,128)} %get-tuple-element.76) | copy-start | bytes 6291460
  114.5 16.1 %copy-start.5 = (f32[4,1024,128]{2,1,0:T(8,128)S(1)}, f32[4,1024,128]{2,1,0:T(8,128)}, u32[]{:S(2)}) copy-start(f32[4,1024,128]{2,1,0:T(8,128)} %copy-done.4) | copy-start | bytes 6291460
  121.2 5.4 %collective-permute-start.3 = (f32[4,4,128]{2,1,0:T(4,128)S(1)}, f32[4,4,128]{2,1,0:T(4,128)S(1)}, u32[]{:S(2)}, u32[]{:S(2)}) collective-permute-start(f32[4,4,128]{2,1,0:T(4,128)S(1)} %get-tuple-element.63), channel_id=1, source_target_pairs={{0,8},{8,16},{16,24},{24,32},{32,40},{40,48},{48,56},{56,64},{64,7... | collective-permute-start | bytes 24584 | tf_op jit(solution)/shard_map/ppermute | solution.py:14
  125.1 5.5 %collective-permute-start.2 = (f32[4,4,128]{2,1,0:T(4,128)S(1)}, f32[4,4,128]{2,1,0:T(4,128)S(1)}, u32[]{:S(2)}, u32[]{:S(2)}) collective-permute-start(f32[4,4,128]{2,1,0:T(4,128)S(1)} %get-tuple-element.62), channel_id=1, source_target_pairs={{8,0},{16,8},{24,16},{32,24},{40,32},{48,40},{56,48},{64,56},{72,6... | collective-permute-start | bytes 24584 | tf_op jit(solution)/shard_map/ppermute | solution.py:17
  133.7 1.0 copy-start.6
  189.7 129.8 %reduce-scatter.17.cloned.1.call-start = ((), (), s32[]{:S(2)}) async-start(), calls=%async_computation.8 | async-start | bytes 557056
  197.1 198.1 %reduce-scatter.13.cloned.1.call-start = ((), (), s32[]{:S(2)}) async-start(), calls=%async_computation.6 | async-start | bytes 557056
  203.1 267.3 %reduce-scatter.15.cloned.1.call-start = ((), (), s32[]{:S(2)}) async-start(), calls=%async_computation.7 | async-start | bytes 557056
  242.4 53.2 %all-to-all-start = ((bf16[4,16,8,1024]{3,2,0,1:T(8,128)(2,1)}), bf16[4,16,8,1024]{3,2,0,1:T(8,128)(2,1)S(1)}, u32[]{:S(2)}, u32[]{:S(2)}) async-start(bf16[4,16,8,1024]{3,2,0,1:T(8,128)(2,1)} %copy.46), calls=%async_computation.1 | async-start | bytes 2097152 | tf_op jit(solution)/shard_map/all_to_all | solution.py:145
  295.6 174.9 %copy-start.1 = (bf16[1024,128]{1,0:T(8,128)(2,1)S(1)}, bf16[1024,128]{1,0:T(8,128)(2,1)}, u32[]{:S(2)}) copy-start(bf16[1024,128]{1,0:T(8,128)(2,1)} %param.12) | copy-start | bytes 786436
Sparse Core Ops, SparseCore 0:
  189.8 49.5 reduce-scatter.10
  243.1 76.2 reduce-scatter.16
  323.5 71.5 reduce-scatter.12
  398.8 71.5 reduce-scatter.14
where the time goes:
time: 478 us; the launch traced here: 477 us
  waiting for transfers between devices  196 us (41%)
  blocking collectives  125 us (26%)
  local copies, waits for them, and re-layouts  54 us (11%)
  matrix products  52.9 us (11%)
  starting transfers between devices  18.6 us (4%)
  other arithmetic  16.3 us (3%)
  between operations  14.7 us (3%)
    unnamed x7, waiting for transfers between devices  173 us
    psum x3, blocking collectives, channel_sums(): return lax.psum(parts, 'seq')  125 us
    convert_element_type x3, local copies, waits for them, and re-layouts, per_device(): channel_partial.astype(jnp.bfloat16)  35.6 us
    reduce_scatter x1, waiting for transfers between devices, per_device(): lax.psum_scatter(channel_partial.astype(jnp.bfloat16), 'tp', scatter_dime...  18.8 us
    unnamed x32, local copies, waits for them, and re-layouts  15.4 us
    dot_general x1, matrix products, per_device(): lax.dot_general(grad_gate, gate_weight, (((1,), (1,)), ((), ())), preferr...  11.3 us
  transfers between devices with their start and end apart: 9, of which 5 were waited for; matrix products, arithmetic and copies ran while one was open for 8% of the time, Pallas kernels for 0%

commit v1 on v0

v1 whole, which is shorter than its diff:
```python
import functools

import jax
import jax.numpy as jnp
from jax import lax
from jax.experimental import pallas as pl
from jax.experimental.pallas import tpu as pltpu
from jax.sharding import PartitionSpec as P

MESH = pl.DeviceIdType.MESH
F32 = jnp.float32
BF16 = jnp.bfloat16
EPS = 1e-05
LANES = 128
EDGE = 8
XN = 4


def mm(a, b):
    return jnp.dot(a, b, preferred_element_type=F32)


def mm_t(a, b):
    return lax.dot_general(a, b, (((1,), (1,)), ((), ())), preferred_element_type=F32)


def mm_tl(a, b):
    return lax.dot_general(a, b, (((0,), (0,)), ((), ())), preferred_element_type=F32)


def fold(v):
    rows = v.shape[0]
    return jnp.sum(v.reshape(rows // 8, 8, LANES), axis=0)


def kernel(
    cfg,
    lengths,
    normed_h,
    grads_h,
    wv_h,
    wg_h,
    wo_h,
    taps,
    gain,
    shift,
    gin,
    gwv,
    gwg,
    gwo,
    gtaps,
    ggain,
    gshift,
    nv,
    gv,
    wcat,
    wo,
    wd_own,
    wd_send,
    wd_oth,
    gp,
    gs,
    a2,
    cv,
    gn,
    gc,
    sw,
    halo,
    red_a,
    red_b,
    red_c,
    got,
    gbuf,
    goth,
    s2,
    r2,
    sx,
    rx,
    osend,
    tacc,
    wacc,
    woacc,
    wsend,
    wrecv,
    load_sem,
    halo_send,
    halo_recv,
    red_send,
    red_recv,
    wx_send,
    wx_recv,
    ge_send,
    ge_recv,
    d2_send,
    d2_recv,
    nb_send,
    nb_recv,
    aa_send,
    aa_recv,
    aa_own,
    wr_send,
    wr_recv,
):
    R, NF, D, NS, F, TM, TC = cfg
    K = taps.shape[0]
    H = (K - 1) // 2
    M = 8 * NS
    NCH = R * NF // F
    cpr = NF // F
    HF = F // 2
    DP = D // NS
    s = lax.axis_index("seq")
    t = lax.axis_index("tp")
    x = lax.div(t, 2)
    core = lax.rem(t, 2)
    other = x * 2 + (1 - core)
    right = lax.rem(x + 1, XN) * 2 + core
    left = lax.rem(x + XN - 1, XN) * 2 + core
    up = lax.rem(s + 1, NS)
    down = lax.rem(s + NS - 1, NS)

    barrier = pltpu.get_barrier_semaphore()

    def greet(k, carry):
        pl.semaphore_signal(
            barrier, inc=1, device_id=(lax.rem(s + k, NS), t), device_id_type=MESH
        )
        return carry

    lax.fori_loop(1, NS, greet, 0)
    for mate in (other, right, left):
        pl.semaphore_signal(barrier, inc=1, device_id=(s, mate), device_id_type=MESH)

    loads = [
        pltpu.make_async_copy(wv_h, wcat.at[:, 0:LANES], load_sem.at[0]),
        pltpu.make_async_copy(wg_h, wcat.at[:, LANES : 2 * LANES], load_sem.at[1]),
        pltpu.make_async_copy(wo_h, wo, load_sem.at[2]),
    ]
    for load in loads:
        load.start()

    def normed_load(r):
        return pltpu.make_async_copy(normed_h.at[r], nv.at[r], load_sem.at[3 + r])

    def grads_load(r):
        return pltpu.make_async_copy(grads_h.at[r], gv.at[r], load_sem.at[3 + R + r])

    for r in range(R):
        normed_load(r).start()
    for r in range(R):
        grads_load(r).start()

    def valid(r, row0, rows):
        at = s * NF + row0 + lax.broadcasted_iota(jnp.int32, (rows, LANES), 0)
        return jnp.logical_and(at >= 0, at < lengths[r])

    def picker(xd, cd):
        row = lax.broadcasted_iota(jnp.int32, (M, D), 0)
        col = lax.broadcasted_iota(jnp.int32, (M, D), 1)
        want = (row // 8) * 64 + xd * 16 + cd * 8 + row % 8
        return jnp.where(col == want, 1.0, 0.0).astype(BF16)

    loads[0].wait()
    loads[1].wait()

    def pick_weights(xd, carry):
        rows = pl.ds(pl.multiple_of(xd * M, M), M)
        wd_own[rows, :] = mm(picker(xd, core), wcat[...]).astype(BF16)
        wd_send[rows, :] = mm(picker(xd, 1 - core), wcat[...]).astype(BF16)
        return carry

    lax.fori_loop(0, XN, pick_weights, 0)
    tacc[...] = jnp.zeros_like(tacc)
    wacc[...] = jnp.zeros_like(wacc)
    woacc[...] = jnp.zeros_like(woacc)

    pl.semaphore_wait(barrier, NS - 1 + 3)

    def remote(src, dst, send, recv, device):
        return pltpu.make_async_remote_copy(
            src_ref=src,
            dst_ref=dst,
            send_sem=send,
            recv_sem=recv,
            device_id=device,
            device_id_type=MESH,
        )

    weight_swap = remote(wd_send, wd_oth, wx_send, wx_recv, (s, other))
    weight_swap.start()

    def edge_copies(kind, field, r):
        index = kind * 2 * R + 2 * r
        return (
            remote(
                field.at[r, pl.ds(NF, EDGE)],
                halo.at[kind, r, 0],
                halo_send.at[index],
                halo_recv.at[index],
                (up, t),
            ),
            remote(
                field.at[r, pl.ds(EDGE, EDGE)],
                halo.at[kind, r, 1],
                halo_send.at[index + 1],
                halo_recv.at[index + 1],
                (down, t),
            ),
        )

    def send_edges(kind, field, r):
        for copy in edge_copies(kind, field, r):
            copy.start()

    def take_edges(kind, field, r):
        low, high = edge_copies(kind, field, r)
        low.wait_recv()
        high.wait_recv()
        field[r, 0:EDGE] = jnp.where(s > 0, halo[kind, r, 0], 0.0)
        field[r, NF + EDGE : NF + 2 * EDGE] = jnp.where(s < NS - 1, halo[kind, r, 1], 0.0)

    per_rec = NF // TM

    def forward(i, carry):
        r = lax.div(i, per_rec)
        part = lax.rem(i, per_rec)
        row0 = pl.multiple_of(part * TM, TM)
        rows = pl.ds(row0, TM)

        @pl.when(part == 0)
        def _():
            normed_load(r).wait()

        both = mm(nv[r, rows, :], wcat[...])
        gate = jax.nn.sigmoid(both[:, LANES:])
        unit = both[:, :LANES] * gate
        gp[r, pl.ds(row0 + EDGE, TM)] = jnp.where(valid(r, row0, TM), unit, 0.0)
        gs[r, rows] = gate
        a2[r, rows] = unit * (1.0 - gate)

        @pl.when(part == per_rec - 1)
        def _():
            send_edges(0, gp, r)

        return carry

    lax.fori_loop(0, R * per_rec, forward, 0)

    tap_rows = [taps[k : k + 1, :] for k in range(K)]
    tiles = NF // TC
    zero = jnp.zeros((8, LANES), F32)

    def conv_rec(r, sums):
        take_edges(0, gp, r)

        def conv_tile(i, sums):
            row0 = pl.multiple_of(i * TC, TC)
            total = tap_rows[0] * gp[r, pl.ds(row0 + EDGE - H, TC)]
            for k in range(1, K):
                total = total + tap_rows[k] * gp[r, pl.ds(row0 + EDGE - H + k, TC)]
            cv[r, pl.ds(row0 + EDGE, TC)] = total
            kept = jnp.where(valid(r, row0, TC), total, 0.0)
            return sums[0] + fold(kept), sums[1] + fold(kept * kept)

        sums = lax.fori_loop(0, tiles, conv_tile, sums)
        send_edges(1, cv, r)
        return sums

    sums = lax.fori_loop(0, R, conv_rec, (zero, zero))

    def red_wait(red, index):
        part = red.at[pl.ds(0, NS - 1)]
        pltpu.make_async_copy(part, part, red_recv.at[index]).wait()

    def red_sent(red, index):
        part = red.at[pl.ds(0, NS - 1)]
        pltpu.make_async_copy(part, part, red_send.at[index]).wait()

    def spread(red, index, value):
        red[s] = value

        def give(k, carry):
            remote(
                red.at[s], red.at[s], red_send.at[index], red_recv.at[index], (lax.rem(s + k, NS), t)
            ).start()
            return carry

        lax.fori_loop(1, NS, give, 0)

    def two_rows(first, second):
        row = lax.broadcasted_iota(jnp.int32, (8, LANES), 0)
        first = jnp.sum(first, axis=0, keepdims=True)
        second = jnp.sum(second, axis=0, keepdims=True)
        return jnp.where(row == 0, first, jnp.where(row == 1, second, 0.0))

    def collect(red, index):
        red_wait(red, index)
        total = red[0]
        for k in range(1, NS):
            total = total + red[k]
        return total

    spread(red_a, 0, two_rows(*sums))

    loads[2].wait()

    def back_one(i, carry):
        r = lax.div(i, per_rec)
        part = lax.rem(i, per_rec)
        row0 = pl.multiple_of(part * TM, TM)

        @pl.when(part == 0)
        def _():
            grads_load(r).wait()

        gn[r, pl.ds(row0 + EDGE, TM)] = mm(gv[r, pl.ds(row0, TM), :], wo[...])
        return carry

    lax.fori_loop(0, R * per_rec, back_one, 0)

    total = collect(red_a, 0)
    count = (lengths[0] + lengths[1] + lengths[2] + lengths[3]).astype(F32)
    inv_count = 1.0 / jnp.full((1, LANES), count, F32)
    centre = total[0:1] * inv_count
    spread_sq = total[1:2] * inv_count - centre * centre
    inv_std = lax.rsqrt(spread_sq + EPS)
    gain_row = gain[...]
    shift_row = shift[...]

    def norm_rec(r, sums):
        def norm_tile(i, sums):
            row0 = pl.multiple_of(i * TC, TC)
            rows = pl.ds(row0, TC)
            padded = pl.ds(row0 + EDGE, TC)
            unit = (cv[r, padded] - centre) * inv_std
            normalized = unit * gain_row + shift_row
            sig = jax.nn.sigmoid(normalized)
            ok = valid(r, row0, TC)
            sw[r, rows] = jnp.where(ok, normalized * sig, 0.0).astype(BF16)
            grad = gn[r, padded] * sig * (1.0 + normalized * (1.0 - sig))
            grad = jnp.where(ok, grad, 0.0)
            gn[r, padded] = grad
            return sums[0] + fold(grad), sums[1] + fold(grad * unit)

        sums = lax.fori_loop(0, tiles, norm_tile, sums)
        send_edges(2, gn, r)
        return sums

    sums = lax.fori_loop(0, R, norm_rec, (zero, zero))
    spread(red_b, 1, two_rows(*sums))

    own_pick = picker(x, core)

    def chunk_place(q):
        r = lax.div(q, cpr)
        return r, pl.multiple_of(lax.rem(q, cpr) * F, F)

    def out_weight_part(q, carry):
        r, row0 = chunk_place(q)
        rows = pl.ds(row0, F)
        woacc[...] += mm_tl(sw[r, rows, :], gv[r, rows, :])
        got[q] = mm_t(own_pick, gv[r, rows, :]).astype(BF16)
        return carry

    lax.fori_loop(0, NCH, out_weight_part, 0)

    def ship_weight(index, acc, first):
        for b in range(D // LANES):
            wsend[index, b * LANES : (b + 1) * LANES, :] = jnp.transpose(
                acc[first : first + LANES, b * LANES : (b + 1) * LANES]
            )

        def give(k, carry):
            p = lax.rem(s + k, NS)
            remote(
                wsend.at[index, pl.ds(pl.multiple_of(p * DP, DP), DP)],
                wrecv.at[index, s],
                wr_send.at[index],
                wr_recv.at[index],
                (p, t),
            ).start()
            return carry

        lax.fori_loop(1, NS, give, 0)
        wrecv[index, s] = wsend[index, pl.ds(pl.multiple_of(s * DP, DP), DP)]

    ship_weight(2, woacc, 0)

    total = collect(red_b, 1)
    gshift[...] = total[0:1]
    ggain[...] = total[1:2]
    scale = gain_row * inv_std
    mean_shift = total[0:1] * inv_count
    mean_gain = total[1:2] * inv_count

    padded_rows = NF + 2 * EDGE
    TE = padded_rows // 10 if padded_rows % 80 == 0 else 8

    def conv_grad_rec(r, carry):
        take_edges(1, cv, r)
        take_edges(2, gn, r)

        def conv_grad_tile(i, carry):
            row0 = pl.multiple_of(i * TE, TE)
            rows = pl.ds(row0, TE)
            unit = (cv[r, rows] - centre) * inv_std
            grad = scale * (gn[r, rows] - mean_shift - unit * mean_gain)
            gc[r, rows] = jnp.where(valid(r, row0 - EDGE, TE), grad, 0.0)
            return carry

        return lax.fori_loop(0, padded_rows // TE, conv_grad_tile, carry)

    lax.fori_loop(0, R, conv_grad_rec, 0)
    weight_swap.wait_recv()

    def swap_copy(q):
        return remote(gbuf.at[q], goth.at[q], ge_send.at[q], ge_recv.at[q], (s, other))

    def d2_copies(q):
        return (
            remote(s2.at[q, 0], r2.at[q, 0], d2_send.at[2 * q], d2_recv.at[2 * q], (s, right)),
            remote(
                s2.at[q, 1], r2.at[q, 1], d2_send.at[2 * q + 1], d2_recv.at[2 * q + 1], (s, left)
            ),
        )

    def nb_copies(q):
        return (
            remote(sx.at[q, 0], rx.at[q, 0], nb_send.at[2 * q], nb_recv.at[2 * q], (s, right)),
            remote(
                sx.at[q, 1], rx.at[q, 1], nb_send.at[2 * q + 1], nb_recv.at[2 * q + 1], (s, left)
            ),
        )

    def weight_rows(hop):
        return pl.ds(pl.multiple_of(lax.rem(x + hop, XN) * M, M), M)

    def partial(q, hop):
        rows = weight_rows(hop)
        return mm_t(wd_own[rows, :], gbuf[q]) + mm_t(wd_oth[rows, :], goth[q])

    def pointwise_grads(q):
        r, base = chunk_place(q)

        def tile(i, taps_sum):
            row0 = pl.multiple_of(base + i * TC, TC)
            rows = pl.ds(row0, TC)
            here = pl.ds(pl.multiple_of(i * TC, TC), TC)
            grad = tap_rows[0] * gc[r, pl.ds(row0 + EDGE + H, TC)]
            for k in range(1, K):
                grad = grad + tap_rows[k] * gc[r, pl.ds(row0 + EDGE + H - k, TC)]
            grad = jnp.where(valid(r, row0, TC), grad, 0.0)
            gbuf[q, here, 0:LANES] = (grad * gs[r, rows]).astype(BF16)
            gbuf[q, here, LANES : 2 * LANES] = (grad * a2[r, rows]).astype(BF16)
            centre_rows = gc[r, pl.ds(row0 + EDGE, TC)]
            return tuple(
                taps_sum[k] + fold(centre_rows * gp[r, pl.ds(row0 + EDGE - H + k, TC)])
                for k in range(K)
            )

        taps_sum = lax.fori_loop(0, F // TC, tile, tuple(tacc[k] for k in range(K)))
        for k in range(K):
            tacc[k] = taps_sum[k]

    def far_sends(q):
        swap_copy(q).wait_recv()
        far = partial(q, 2).astype(BF16)
        s2[q, 0] = far[:, :HF]
        s2[q, 1] = far[:, HF:]
        for copy in d2_copies(q):
            copy.start()

    def near_sends(q):
        to_right = partial(q, 1)
        to_left = partial(q, 3)
        from_left, from_right = d2_copies(q)
        from_left.wait_recv()
        sx[q, 0, :, :HF] = (to_right[:, :HF] + r2[q, 0].astype(F32)).astype(BF16)
        sx[q, 0, :, HF:] = to_right[:, HF:].astype(BF16)
        from_right.wait_recv()
        sx[q, 1, :, :HF] = to_left[:, :HF].astype(BF16)
        sx[q, 1, :, HF:] = (to_left[:, HF:] + r2[q, 1].astype(F32)).astype(BF16)
        for copy in nb_copies(q):
            copy.start()

    def out_place(q, owner):
        r, row0 = chunk_place(q)
        return gin.at[r, :, pl.ds(pl.multiple_of(owner * NF + row0, F), F)]

    def own_copy(q):
        return pltpu.make_async_copy(osend.at[q, s], out_place(q, s), aa_own.at[q])

    def finish(q):
        total = partial(q, 0) + got[q].astype(F32)
        for copy in nb_copies(q):
            copy.wait_recv()
        total = total + rx[q, 0].astype(F32) + rx[q, 1].astype(F32)
        osend[q] = total.astype(BF16).reshape(NS, 8, F)
        own_copy(q).start()

        def give(k, carry):
            p = lax.rem(s + k, NS)
            remote(
                osend.at[q, p], out_place(q, s), aa_send.at[q], aa_recv.at[q], (p, t)
            ).start()
            return carry

        lax.fori_loop(1, NS, give, 0)

    def weight_part(q):
        r, row0 = chunk_place(q)
        wacc[...] += mm_tl(gbuf[q], nv[r, pl.ds(row0, F), :])

    LAG_A, LAG_B, LAG_C = 1, 2, 4

    def step(i, carry):
        @pl.when(i < NCH)
        def _():
            pointwise_grads(i)
            swap_copy(i).start()

        @pl.when(jnp.logical_and(i >= LAG_A, i < NCH + LAG_A))
        def _():
            far_sends(i - LAG_A)

        @pl.when(i < NCH)
        def _():
            weight_part(i)

        @pl.when(i == NCH - 1)
        def _():
            for k in range(K):
                red_c[s, k : k + 1] = jnp.sum(tacc[k], axis=0, keepdims=True)

            def give(k, carry):
                remote(
                    red_c.at[s], red_c.at[s], red_send.at[2], red_recv.at[2], (lax.rem(s + k, NS), t)
                ).start()
                return carry

            lax.fori_loop(1, NS, give, 0)
            ship_weight(0, wacc, 0)
            ship_weight(1, wacc, LANES)

        @pl.when(jnp.logical_and(i >= LAG_B, i < NCH + LAG_B))
        def _():
            near_sends(i - LAG_B)

        @pl.when(i >= LAG_C)
        def _():
            finish(i - LAG_C)

        return carry

    for k in range(K, 16):
        red_c[s, k : k + 1] = jnp.zeros((1, LANES), F32)
    lax.fori_loop(0, NCH + LAG_C, step, 0)

    gtaps[...] = collect(red_c, 2)[0:K]

    for index, out in ((2, gwo), (0, gwv), (1, gwg)):
        slots = wrecv.at[index, pl.ds(0, NS - 1)]
        pltpu.make_async_copy(slots, slots, wr_recv.at[index]).wait()
        total = wrecv[index, 0]
        for k in range(1, NS):
            total = total + wrecv[index, k]
        out[...] = total

    weight_swap.wait_send()

    def edges_left(index, carry):
        part = halo.at[0, 0, 0]
        pltpu.make_async_copy(part, part, halo_send.at[index]).wait()
        return carry

    lax.fori_loop(0, 6 * R, edges_left, 0)
    red_sent(red_a, 0)
    red_sent(red_b, 1)
    red_sent(red_c, 2)
    for index in range(3):
        slots = wrecv.at[index, pl.ds(0, NS - 1)]
        pltpu.make_async_copy(slots, slots, wr_send.at[index]).wait()

    def drain(q, carry):
        swap_copy(q).wait_send()
        for copy in d2_copies(q):
            copy.wait_send()
        for copy in nb_copies(q):
            copy.wait_send()
        own_copy(q).wait()
        part = osend.at[q, pl.ds(0, NS - 1)]
        pltpu.make_async_copy(part, part, aa_send.at[q]).wait()
        pltpu.make_async_copy(part, part, aa_recv.at[q]).wait()
        return carry

    lax.fori_loop(0, NCH, drain, 0)


def per_device(
    normed,
    grad_out,
    value_weight,
    gate_weight,
    depth_taps,
    norm_gain,
    norm_shift,
    out_weight,
    lengths,
):
    R, NF, D = normed.shape
    K, CW = depth_taps.shape
    NS = lax.axis_size("seq")
    M = 8 * NS
    F = min(512, NF)
    TM = min(512, NF)
    TC = min(64, F)
    NCH = R * NF // F
    HF = F // 2
    DP = D // NS
    cfg = (R, NF, D, NS, F, TM, TC)
    vmem = pl.BlockSpec(memory_space=pltpu.VMEM)
    hbm = pl.BlockSpec(memory_space=pl.ANY)
    dma = pltpu.SemaphoreType.DMA
    padded = NF + 2 * EDGE
    out_shape = (
        jax.ShapeDtypeStruct((R, 8, NS * NF), BF16),
        jax.ShapeDtypeStruct((DP, CW), F32),
        jax.ShapeDtypeStruct((DP, CW), F32),
        jax.ShapeDtypeStruct((DP, CW), F32),
        jax.ShapeDtypeStruct((K, CW), F32),
        jax.ShapeDtypeStruct((1, CW), F32),
        jax.ShapeDtypeStruct((1, CW), F32),
    )
    scratch = [
        pltpu.VMEM((R, NF, D), BF16),
        pltpu.VMEM((R, NF, D), BF16),
        pltpu.VMEM((D, 2 * LANES), BF16),
        pltpu.VMEM((D, LANES), BF16),
        pltpu.VMEM((XN * M, 2 * LANES), BF16),
        pltpu.VMEM((XN * M, 2 * LANES), BF16),
        pltpu.VMEM((XN * M, 2 * LANES), BF16),
        pltpu.VMEM((R, padded, LANES), F32),
        pltpu.VMEM((R, NF, LANES), F32),
        pltpu.VMEM((R, NF, LANES), F32),
        pltpu.VMEM((R, padded, LANES), F32),
        pltpu.VMEM((R, padded, LANES), F32),
        pltpu.VMEM((R, padded, LANES), F32),
        pltpu.VMEM((R, NF, LANES), BF16),
        pltpu.VMEM((3, R, 2, EDGE, LANES), F32),
        pltpu.VMEM((NS, 8, LANES), F32),
        pltpu.VMEM((NS, 8, LANES), F32),
        pltpu.VMEM((NS, 16, LANES), F32),
        pltpu.VMEM((NCH, M, F), BF16),
        pltpu.VMEM((NCH, F, 2 * LANES), BF16),
        pltpu.VMEM((NCH, F, 2 * LANES), BF16),
        pltpu.VMEM((NCH, 2, M, HF), BF16),
        pltpu.VMEM((NCH, 2, M, HF), BF16),
        pltpu.VMEM((NCH, 2, M, F), BF16),
        pltpu.VMEM((NCH, 2, M, F), BF16),
        pltpu.VMEM((NCH, NS, 8, F), BF16),
        pltpu.VMEM((K, 8, LANES), F32),
        pltpu.VMEM((2 * LANES, D), F32),
        pltpu.VMEM((LANES, D), F32),
        pltpu.VMEM((3, D, LANES), F32),
        pltpu.VMEM((3, NS, DP, LANES), F32),
        dma((3 + 2 * R,)),
        dma((6 * R,)),
        dma((6 * R,)),
        dma((3,)),
        dma((3,)),
        dma,
        dma,
        dma((NCH,)),
        dma((NCH,)),
        dma((2 * NCH,)),
        dma((2 * NCH,)),
        dma((2 * NCH,)),
        dma((2 * NCH,)),
        dma((NCH,)),
        dma((NCH,)),
        dma((NCH,)),
        dma((3,)),
        dma((3,)),
    ]
    outs = pl.pallas_call(
        functools.partial(kernel, cfg),
        out_shape=out_shape,
        in_specs=[pl.BlockSpec(memory_space=pltpu.SMEM)] + [hbm] * 5 + [vmem] * 3,
        out_specs=(hbm,) + (vmem,) * 6,
        scratch_shapes=scratch,
        compiler_params=pltpu.CompilerParams(
            collective_id=0, has_side_effects=True, vmem_limit_bytes=60 * 1024 * 1024
        ),
        cost_estimate=pl.CostEstimate(
            flops=8 * 2 * R * NF * D * CW, bytes_accessed=4 * R * NF * D, transcendentals=0
        ),
    )(
        lengths,
        normed,
        grad_out,
        value_weight,
        gate_weight,
        out_weight,
        depth_taps,
        norm_gain.reshape(1, CW),
        norm_shift.reshape(1, CW),
    )
    grad_in, grad_wv, grad_wg, grad_wo, grad_taps, grad_gain, grad_shift = outs
    return (
        grad_in,
        grad_wv,
        grad_wg,
        grad_wo,
        grad_taps,
        grad_gain.reshape(CW),
        grad_shift.reshape(CW),
    )


def solution(mesh):
    placed = (
        P(None, "seq", None),
        P(None, "seq", None),
        P(None, "tp"),
        P(None, "tp"),
        P(None, "tp"),
        P("tp"),
        P("tp"),
        P(None, "tp"),
        P(),
    )
    return jax.shard_map(
        per_device,
        mesh=mesh,
        in_specs=placed,
        out_specs=(
            P(None, ("seq", "tp"), None),
            P("seq", "tp"),
            P("seq", "tp"),
            P("seq", "tp"),
            P(None, "tp"),
            P("tp"),
            P("tp"),
        ),
        check_vma=False,
    )
```

time: 478 us -> 89.9 us (0.19)
  waiting for transfers between devices: 196 us -> 0 us
  blocking collectives: 125 us -> 0 us
  Pallas kernels: 0 us -> 78.8 us
  matrix products: 52.9 us -> 0 us
  local copies, waits for them, and re-layouts: 54 us -> 9.98 us
  starting transfers between devices: 18.6 us -> 0 us
  other arithmetic: 16.3 us -> 0 us
  between operations: 14.7 us -> 0.65 us
    unnamed x7 -> x0, waiting for transfers between devices: 173 us -> none
    psum x3 -> x0, blocking collectives: 125 us -> none  [channel_sums(): return lax.psum(parts, 'seq')]
    pallas_call x0 -> x1, Pallas kernels: none -> 78.8 us  [per_device(): pl.pallas_call(functools.partial(kernel, cfg), out_shape=out_shape, in_sp...]
    dot_general x8 -> x0, matrix products: 52.9 us -> none  [the longest x1 11.3 us: per_device(): lax.dot_general(grad_gate, gate_weight, (((1,), (1,)), ((), ())), preferr...]
    convert_element_type x4 -> x0, local copies, waits for them, and re-layouts: 36.7 us -> none  [the longest x3 35.6 us: per_device(): channel_partial.astype(jnp.bfloat16)]
    reduce_scatter x1 -> x0, waiting for transfers between devices: 18.8 us -> none  [per_device(): lax.psum_scatter(channel_partial.astype(jnp.bfloat16), 'tp', scatter_dime...]
    ppermute x4 -> x0, starting transfers between devices: 11.2 us -> none  [the longest x2 8.46 us: extended(): lax.ppermute(lax.slice_in_dim(block, block.shape[dim] - width, None, axis...]
    reduce_sum x3 -> x0, other arithmetic: 11 us -> none  [the longest x1 6.58 us: per_device(): tap_list.append(jnp.sum(grad_conv * window, axis=(0, 1)))]
  transfers between devices with their start and end apart: 9 -> 0, of which waited for: 5 -> 0; matrix products, arithmetic and copies ran while one was open for 8% -> 0% of each run, Pallas kernels for 0% -> 0%
where the time goes in v1:
time: 89.9 us; the launch traced here: 89.4 us
  Pallas kernels  78.8 us (88%)
  local copies, waits for them, and re-layouts  9.98 us (11%)
    pallas_call x1, Pallas kernels, per_device(): pl.pallas_call(functools.partial(kernel, cfg), out_shape=out_shape, in_sp...  78.8 us
    unnamed x7, local copies, waits for them, and re-layouts  9.98 us

profile of v1, /device:TPU:0, one launch (start us, length us, event | category | flops | bytes accessed | tf_op | source)
XLA Modules:
  0.0 89.4 jit_solution(3860149579540769475)
XLA Ops:
  0.6 78.8 %shard_map.144 = (bf16[4,8,16384]{2,1,0:T(8,128)(2,1)}, f32[64,128]{1,0:T(8,128)}, f32[64,128]{1,0:T(8,128)}, f32[64,128]{1,0:T(8,128)}, f32[9,128]{1,0:T(8,128)}, /*index=5*/f32[1,128]{1,0:T(1,128)}, f32[1,128]{1,0:T(1,128)}) custom-call(s32[4]{0:T(128)} %lengths.1, bf16[4,1024,1024]{2,1,0:T(8,128)(2,1)} %normed_h.1, bf16[4,1024,1024]{2,1,0:T(8,128)(2,1)} %grads_h.1, ...), custom_call_target="tpu_custom_call" | custom-call | flops 8589934592 | bytes 16777216 | tf_op jit(solution)/shard_map/pallas_call | solution.py:685
  79.4 2.3 %copy.23 = bf16[4,8,16384]{2,1,0:T(8,128)(2,1)} copy(bf16[4,8,16384]{2,1,0:T(8,128)(2,1)} %get-tuple-element.28) | data formatting | bytes 2097152
  81.7 1.4 %copy.24 = f32[64,128]{1,0:T(8,128)} copy(f32[64,128]{1,0:T(8,128)} %get-tuple-element.29) | data formatting | bytes 65536
  83.1 1.4 %copy.25 = f32[64,128]{1,0:T(8,128)} copy(f32[64,128]{1,0:T(8,128)} %get-tuple-element.30) | data formatting | bytes 65536
  84.4 1.4 %copy.26 = f32[64,128]{1,0:T(8,128)} copy(f32[64,128]{1,0:T(8,128)} %get-tuple-element.31) | data formatting | bytes 65536
  85.8 1.3 %copy.27 = f32[9,128]{1,0:T(8,128)} copy(f32[9,128]{1,0:T(8,128)} %get-tuple-element.32) | data formatting | bytes 9216
  87.1 1.2 %copy.28 = f32[128]{0:T(128)} copy(f32[128]{0:T(128)} %bitcast.7) | data formatting | bytes 1024
  88.3 1.1 %copy.29 = f32[128]{0:T(128)} copy(f32[128]{0:T(128)} %bitcast.6) | data formatting | bytes 1024

commit v2 on v1

v2 whole, which is shorter than its diff:
```python
import functools

import jax
import jax.numpy as jnp
from jax import lax
from jax.experimental import pallas as pl
from jax.experimental.pallas import tpu as pltpu
from jax.sharding import PartitionSpec as P

MESH = pl.DeviceIdType.MESH
F32 = jnp.float32
BF16 = jnp.bfloat16
EPS = 1e-05
LANES = 128
EDGE = 8
PAD = 16
XN = 4


def mm(a, b):
    return jnp.dot(a, b, preferred_element_type=F32)


def mm_t(a, b):
    return lax.dot_general(a, b, (((1,), (1,)), ((), ())), preferred_element_type=F32)


def mm_tl(a, b):
    return lax.dot_general(a, b, (((0,), (0,)), ((), ())), preferred_element_type=F32)


def fold(v):
    rows = v.shape[0]
    return jnp.sum(v.reshape(rows // 8, 8, LANES), axis=0)


def kernel(
    cfg,
    lengths,
    normed_h,
    grads_h,
    wv_h,
    wg_h,
    wo_h,
    taps,
    gain,
    shift,
    gin,
    gwv,
    gwg,
    gwo,
    gtaps,
    ggain,
    gshift,
    nv,
    gv,
    wcat,
    wo,
    w_next,
    pick_own,
    wd,
    wd_send,
    gp,
    gs,
    a2,
    cv,
    gn,
    gc,
    sw,
    halo_out,
    halo,
    red_a,
    red_b,
    red_c,
    gg_out,
    gg_in,
    gmine,
    gother,
    far_out,
    far_in,
    osend,
    tacc,
    wacc,
    woacc,
    wsend,
    wrecv,
    load_sem,
    halo_send,
    halo_recv,
    red_send,
    red_recv,
    wx_send,
    wx_recv,
    wn_send,
    wn_recv,
    ge_send,
    ge_recv,
    gg_send,
    gg_recv,
    fr_send,
    fr_recv,
    aa_send,
    aa_recv,
    aa_own,
    wr_send,
    wr_recv,
):
    R, NF, D, NS, F, TM, TC = cfg
    K = taps.shape[0]
    H = (K - 1) // 2
    M = 8 * NS
    NCH = R * NF // F
    cpr = NF // F
    DP = D // NS
    s = lax.axis_index("seq")
    t = lax.axis_index("tp")
    x = lax.div(t, 2)
    core = lax.rem(t, 2)
    other = x * 2 + (1 - core)
    step = 1 - 2 * lax.rem(x, 2)
    x_far = lax.rem(x + XN - step, XN)
    pair = (x + step) * 2 + core
    far = x_far * 2 + core
    up = lax.rem(s + 1, NS)
    down = lax.rem(s + NS - 1, NS)

    barrier = pltpu.get_barrier_semaphore()

    def greet(k, carry):
        pl.semaphore_signal(
            barrier, inc=1, device_id=(lax.rem(s + k, NS), t), device_id_type=MESH
        )
        return carry

    lax.fori_loop(1, NS, greet, 0)
    for mate in (other, pair, far):
        pl.semaphore_signal(barrier, inc=1, device_id=(s, mate), device_id_type=MESH)

    loads = [
        pltpu.make_async_copy(wv_h, wcat.at[:, 0:LANES], load_sem.at[0]),
        pltpu.make_async_copy(wg_h, wcat.at[:, LANES : 2 * LANES], load_sem.at[1]),
        pltpu.make_async_copy(wo_h, wo, load_sem.at[2]),
    ]
    for load in loads:
        load.start()

    def normed_load(r):
        return pltpu.make_async_copy(normed_h.at[r], nv.at[r], load_sem.at[3 + r])

    def grads_load(r):
        return pltpu.make_async_copy(grads_h.at[r], gv.at[r], load_sem.at[3 + R + r])

    for r in range(R):
        normed_load(r).start()

    def valid(r, row0, rows):
        at = s * NF + row0 + lax.broadcasted_iota(jnp.int32, (rows, LANES), 0)
        return jnp.logical_and(at >= 0, at < lengths[r])

    def picker(xd, cd):
        row = lax.broadcasted_iota(jnp.int32, (M, D), 0)
        col = lax.broadcasted_iota(jnp.int32, (M, D), 1)
        want = (row // 8) * 64 + xd * 16 + cd * 8 + row % 8
        return jnp.where(col == want, 1.0, 0.0).astype(BF16)

    loads[0].wait()
    loads[1].wait()

    def pick_weights(source, group):
        for side, xd in enumerate((x, x_far)):
            rows = slice(side * M, (side + 1) * M)
            wd[group, rows] = mm(picker(xd, core), source[...]).astype(BF16)
            wd_send[group, rows] = mm(picker(xd, 1 - core), source[...]).astype(BF16)

    def weight_swap(group):
        return remote(
            wd_send.at[group],
            wd.at[2 + group],
            wx_send.at[group],
            wx_recv.at[group],
            (s, other),
        )

    tacc[...] = jnp.zeros_like(tacc)
    wacc[...] = jnp.zeros_like(wacc)
    woacc[...] = jnp.zeros_like(woacc)
    for r in range(R):
        gp[r, 0 : PAD - EDGE] = jnp.zeros((PAD - EDGE, LANES), F32)
        gp[r, NF + PAD + EDGE : NF + 2 * PAD] = jnp.zeros((PAD - EDGE, LANES), F32)

    def remote(src, dst, send, recv, device):
        return pltpu.make_async_remote_copy(
            src_ref=src,
            dst_ref=dst,
            send_sem=send,
            recv_sem=recv,
            device_id=device,
            device_id_type=MESH,
        )

    def edge_copies(kind):
        return (
            remote(
                halo_out.at[kind, 0],
                halo.at[kind, 0],
                halo_send.at[2 * kind],
                halo_recv.at[2 * kind],
                (up, t),
            ),
            remote(
                halo_out.at[kind, 1],
                halo.at[kind, 1],
                halo_send.at[2 * kind + 1],
                halo_recv.at[2 * kind + 1],
                (down, t),
            ),
        )

    def send_edges(kind, field):
        for r in range(R):
            halo_out[kind, 0, r] = field[r, PAD + NF - EDGE : PAD + NF]
            halo_out[kind, 1, r] = field[r, PAD : PAD + EDGE]
        for copy in edge_copies(kind):
            copy.start()

    def take_edges(kind, field):
        for copy in edge_copies(kind):
            copy.wait_recv()
        for r in range(R):
            field[r, PAD - EDGE : PAD] = jnp.where(s > 0, halo[kind, 0, r], 0.0)
            field[r, PAD + NF : PAD + NF + EDGE] = jnp.where(s < NS - 1, halo[kind, 1, r], 0.0)

    per_rec = NF // TM

    def forward(i, carry):
        r = lax.div(i, per_rec)
        part = lax.rem(i, per_rec)
        row0 = pl.multiple_of(part * TM, TM)
        rows = pl.ds(row0, TM)

        @pl.when(part == 0)
        def _():
            normed_load(r).wait()
            grads_load(r).start()

        both = mm(nv[r, rows, :], wcat[...])
        gate = jax.nn.sigmoid(both[:, LANES:])
        unit = both[:, :LANES] * gate
        gp[r, pl.ds(row0 + PAD, TM)] = jnp.where(valid(r, row0, TM), unit, 0.0)
        gs[r, rows] = gate
        a2[r, rows] = unit * (1.0 - gate)
        return carry

    lax.fori_loop(0, R * per_rec, forward, 0)
    pl.semaphore_wait(barrier, NS - 1 + 3)
    send_edges(0, gp)
    next_weights = remote(wcat, w_next, wn_send, wn_recv, (s, pair))
    next_weights.start()

    tap_rows = [taps[k : k + 1, :] for k in range(K)]
    tiles = NF // TC
    zero = jnp.zeros((8, LANES), F32)

    def conv_at(r, start, rows):
        total = tap_rows[0] * gp[r, pl.ds(start + PAD - H, rows)]
        for k in range(1, K):
            total = total + tap_rows[k] * gp[r, pl.ds(start + PAD - H + k, rows)]
        return total

    def conv_tile(r, i, sums):
        row0 = pl.multiple_of(i * TC, TC)
        total = conv_at(r, row0, TC)
        cv[r, pl.ds(row0 + PAD, TC)] = total
        kept = jnp.where(valid(r, row0, TC), total, 0.0)
        return sums[0] + fold(kept), sums[1] + fold(kept * kept)

    def conv_inner(r, sums):
        return lax.fori_loop(1, tiles - 1, functools.partial(conv_tile, r), sums)

    sums = lax.fori_loop(0, R, conv_inner, (zero, zero))
    loads[2].wait()

    def back_one(i, carry):
        r = lax.div(i, per_rec)
        part = lax.rem(i, per_rec)
        row0 = pl.multiple_of(part * TM, TM)

        @pl.when(part == 0)
        def _():
            grads_load(r).wait()

        gn[r, pl.ds(row0 + PAD, TM)] = mm(gv[r, pl.ds(row0, TM), :], wo[...])
        return carry

    lax.fori_loop(0, per_rec, back_one, 0)
    take_edges(0, gp)

    def conv_outer(r, sums):
        sums = conv_tile(r, 0, sums)
        return conv_tile(r, tiles - 1, sums)

    sums = lax.fori_loop(0, R, conv_outer, sums)

    def red_wait(red, index):
        part = red.at[pl.ds(0, NS - 1)]
        pltpu.make_async_copy(part, part, red_recv.at[index]).wait()

    def red_sent(red, index):
        part = red.at[pl.ds(0, NS - 1)]
        pltpu.make_async_copy(part, part, red_send.at[index]).wait()

    def spread_from(red, index):
        def give(k, carry):
            remote(
                red.at[s], red.at[s], red_send.at[index], red_recv.at[index], (lax.rem(s + k, NS), t)
            ).start()
            return carry

        lax.fori_loop(1, NS, give, 0)

    def spread(red, index, value):
        red[s] = value
        spread_from(red, index)

    def two_rows(first, second):
        row = lax.broadcasted_iota(jnp.int32, (8, LANES), 0)
        first = jnp.sum(first, axis=0, keepdims=True)
        second = jnp.sum(second, axis=0, keepdims=True)
        return jnp.where(row == 0, first, jnp.where(row == 1, second, 0.0))

    def collect(red, index):
        red_wait(red, index)
        total = red[0]
        for k in range(1, NS):
            total = total + red[k]
        return total

    spread(red_a, 0, two_rows(*sums))

    for r in range(R):
        cv[r, PAD - EDGE : PAD] = conv_at(r, -EDGE, EDGE)
        cv[r, PAD + NF : PAD + NF + EDGE] = conv_at(r, NF, EDGE)
    def chunk_place(q):
        r = lax.div(q, cpr)
        return r, pl.multiple_of(lax.rem(q, cpr) * F, F)

    lax.fori_loop(per_rec, R * per_rec, back_one, 0)
    pick_weights(wcat, 0)
    weight_swap(0).start()
    pick_own[...] = picker(x, core)

    total = collect(red_a, 0)
    count = (lengths[0] + lengths[1] + lengths[2] + lengths[3]).astype(F32)
    inv_count = 1.0 / jnp.full((1, LANES), count, F32)
    centre = total[0:1] * inv_count
    spread_sq = total[1:2] * inv_count - centre * centre
    inv_std = lax.rsqrt(spread_sq + EPS)
    gain_row = gain[...]
    shift_row = shift[...]

    def norm_rec(r, sums):
        def norm_tile(i, sums):
            row0 = pl.multiple_of(i * TC, TC)
            rows = pl.ds(row0, TC)
            padded = pl.ds(row0 + PAD, TC)
            unit = (cv[r, padded] - centre) * inv_std
            normalized = unit * gain_row + shift_row
            sig = jax.nn.sigmoid(normalized)
            ok = valid(r, row0, TC)
            sw[r, rows] = jnp.where(ok, normalized * sig, 0.0).astype(BF16)
            grad = gn[r, padded] * sig * (1.0 + normalized * (1.0 - sig))
            grad = jnp.where(ok, grad, 0.0)
            gn[r, padded] = grad
            return sums[0] + fold(grad), sums[1] + fold(grad * unit)

        return lax.fori_loop(0, tiles, norm_tile, sums)

    sums = lax.fori_loop(0, R, norm_rec, (zero, zero))
    spread(red_b, 1, two_rows(*sums))
    send_edges(1, gn)

    def out_weight_part(q, carry):
        r, row0 = chunk_place(q)
        rows = pl.ds(row0, F)
        woacc[...] += mm_tl(sw[r, rows, :], gv[r, rows, :])
        return carry

    lax.fori_loop(0, NCH, out_weight_part, 0)

    def turn_weight(index, acc, first):
        for b in range(D // LANES):
            wsend[index, b * LANES : (b + 1) * LANES, :] = jnp.transpose(
                acc[first : first + LANES, b * LANES : (b + 1) * LANES]
            )

    def ship_weight(index):
        def give(k, carry):
            p = lax.rem(s + k, NS)
            remote(
                wsend.at[index, pl.ds(pl.multiple_of(p * DP, DP), DP)],
                wrecv.at[index, s],
                wr_send.at[index],
                wr_recv.at[index],
                (p, t),
            ).start()
            return carry

        lax.fori_loop(1, NS, give, 0)
        wrecv[index, s] = wsend[index, pl.ds(pl.multiple_of(s * DP, DP), DP)]

    turn_weight(2, woacc, 0)
    next_weights.wait_recv()
    pick_weights(w_next, 1)
    weight_swap(1).start()
    total = collect(red_b, 1)
    ship_weight(2)
    gshift[...] = total[0:1]
    ggain[...] = total[1:2]
    scale = gain_row * inv_std
    mean_shift = total[0:1] * inv_count
    mean_gain = total[1:2] * inv_count

    take_edges(1, gn)
    padded_rows = NF + 2 * EDGE
    TE = padded_rows // 10 if padded_rows % 80 == 0 else 8

    def conv_grad(r):
        def conv_grad_tile(i, carry):
            row0 = pl.multiple_of(i * TE, TE)
            rows = pl.ds(row0 + PAD - EDGE, TE)
            unit = (cv[r, rows] - centre) * inv_std
            grad = scale * (gn[r, rows] - mean_shift - unit * mean_gain)
            gc[r, rows] = jnp.where(valid(r, row0 - EDGE, TE), grad, 0.0)
            return carry

        lax.fori_loop(0, padded_rows // TE, conv_grad_tile, 0)

    def swap_copy(q, group):
        index = 2 * q + group
        return remote(
            gmine.at[q, group],
            gother.at[q, group],
            ge_send.at[index],
            ge_recv.at[index],
            (s, other),
        )

    def pair_copy(q):
        return remote(gg_out.at[q], gg_in.at[q], gg_send.at[q], gg_recv.at[q], (s, pair))

    def far_copy(q):
        return remote(far_out.at[q], far_in.at[q], fr_send.at[q], fr_recv.at[q], (s, far))

    def partial(q, side):
        rows = slice(side * M, (side + 1) * M)
        total = mm_t(wd[0, rows], gmine[q, 0]) + mm_t(wd[1, rows], gmine[q, 1])
        return total + (mm_t(wd[2, rows], gother[q, 0]) + mm_t(wd[3, rows], gother[q, 1]))

    def pointwise_grads(q):
        r, base = chunk_place(q)

        def tile(i, taps_sum):
            row0 = pl.multiple_of(base + i * TC, TC)
            rows = pl.ds(row0, TC)
            here = pl.ds(pl.multiple_of(i * TC, TC), TC)
            grad = tap_rows[0] * gc[r, pl.ds(row0 + PAD + H, TC)]
            for k in range(1, K):
                grad = grad + tap_rows[k] * gc[r, pl.ds(row0 + PAD + H - k, TC)]
            grad = jnp.where(valid(r, row0, TC), grad, 0.0)
            gg_out[q, here] = grad.astype(BF16)
            gmine[q, 0, here, 0:LANES] = (grad * gs[r, rows]).astype(BF16)
            gmine[q, 0, here, LANES : 2 * LANES] = (grad * a2[r, rows]).astype(BF16)
            centre_rows = gc[r, pl.ds(row0 + PAD, TC)]
            return tuple(
                taps_sum[k] + fold(centre_rows * gp[r, pl.ds(row0 + PAD - H + k, TC)])
                for k in range(K)
            )

        taps_sum = lax.fori_loop(0, F // TC, tile, tuple(tacc[k] for k in range(K)))
        for k in range(K):
            tacc[k] = taps_sum[k]

    def pair_grads(q):
        r, row0 = chunk_place(q)
        both = mm(nv[r, pl.ds(row0, F), :], w_next[...])
        gate = jax.nn.sigmoid(both[:, LANES:])
        unit = both[:, :LANES] * gate
        pair_copy(q).wait_recv()
        grad = gg_in[q].astype(F32)
        gmine[q, 1, :, 0:LANES] = (grad * gate).astype(BF16)
        gmine[q, 1, :, LANES : 2 * LANES] = (grad * (unit * (1.0 - gate))).astype(BF16)
        swap_copy(q, 1).start()

    def far_sends(q):
        for group in range(2):
            swap_copy(q, group).wait_recv()
        far_out[q] = partial(q, 1).astype(BF16)
        far_copy(q).start()

    def out_place(q, owner):
        r, row0 = chunk_place(q)
        return gin.at[r, :, pl.ds(pl.multiple_of(owner * NF + row0, F), F)]

    def own_copy(q):
        return pltpu.make_async_copy(osend.at[q, s], out_place(q, s), aa_own.at[q])

    def finish(q):
        r, row0 = chunk_place(q)
        total = partial(q, 0) + mm_t(pick_own[...], gv[r, pl.ds(row0, F), :])
        far_copy(q).wait_recv()
        total = total + far_in[q].astype(F32)
        osend[q] = total.astype(BF16).reshape(NS, 8, F)
        own_copy(q).start()

        def give(k, carry):
            p = lax.rem(s + k, NS)
            remote(
                osend.at[q, p], out_place(q, s), aa_send.at[q], aa_recv.at[q], (p, t)
            ).start()
            return carry

        lax.fori_loop(1, NS, give, 0)

    def weight_part(q):
        r, row0 = chunk_place(q)
        wacc[...] += mm_tl(gmine[q, 0], nv[r, pl.ds(row0, F), :])

    for k in range(K, 16):
        red_c[s, k : k + 1] = jnp.zeros((1, LANES), F32)

    LATE = NCH // 4

    def outward(i, carry):
        @pl.when(lax.rem(i, cpr) == 0)
        def _():
            conv_grad(lax.div(i, cpr))

        pointwise_grads(i)
        pair_copy(i).start()
        swap_copy(i, 0).start()

        @pl.when(i < NCH - 2 * LATE)
        def _():
            weight_part(i)

        return carry

    lax.fori_loop(0, NCH, outward, 0)
    for group in range(2):
        weight_swap(group).wait_recv()

    LAG_B, LAG_C = 1, 3

    def homeward(i, carry):
        @pl.when(i < NCH)
        def _():
            pair_grads(i)

        @pl.when(jnp.logical_and(i >= LAG_B, i < NCH + LAG_B))
        def _():
            far_sends(i - LAG_B)

        @pl.when(i < LATE)
        def _():
            weight_part(NCH - 2 * LATE + 2 * i)
            weight_part(NCH - 2 * LATE + 2 * i + 1)

        @pl.when(i == LATE - 1)
        def _():
            for index in range(2):
                turn_weight(index, wacc, index * LANES)
                ship_weight(index)
            for k in range(K):
                red_c[s, k : k + 1] = jnp.sum(tacc[k], axis=0, keepdims=True)
            spread_from(red_c, 2)

        @pl.when(i >= LAG_C)
        def _():
            finish(i - LAG_C)

        return carry

    lax.fori_loop(0, NCH + LAG_C, homeward, 0)

    gtaps[...] = collect(red_c, 2)[0:K]

    for index, out in ((2, gwo), (0, gwv), (1, gwg)):
        slots = wrecv.at[index, pl.ds(0, NS - 1)]
        pltpu.make_async_copy(slots, slots, wr_recv.at[index]).wait()
        total = wrecv[index, 0]
        for k in range(1, NS):
            total = total + wrecv[index, k]
        out[...] = total

    next_weights.wait_send()
    for group in range(2):
        weight_swap(group).wait_send()

    for kind in range(2):
        for copy in edge_copies(kind):
            copy.wait_send()
    red_sent(red_a, 0)
    red_sent(red_b, 1)
    red_sent(red_c, 2)
    for index in range(3):
        slots = wrecv.at[index, pl.ds(0, NS - 1)]
        pltpu.make_async_copy(slots, slots, wr_send.at[index]).wait()

    def drain(q, carry):
        for group in range(2):
            swap_copy(q, group).wait_send()
        pair_copy(q).wait_send()
        far_copy(q).wait_send()
        own_copy(q).wait()
        part = osend.at[q, pl.ds(0, NS - 1)]
        pltpu.make_async_copy(part, part, aa_send.at[q]).wait()
        pltpu.make_async_copy(part, part, aa_recv.at[q]).wait()
        return carry

    lax.fori_loop(0, NCH, drain, 0)


def hand_on(*refs):
    half = (len(refs) - 1) // 2
    sems = refs[-1]
    copies = [pltpu.make_async_copy(refs[i], refs[half + i], sems.at[i]) for i in range(half)]
    for copy in copies:
        copy.start()
    for copy in copies:
        copy.wait()


def per_device(
    normed,
    grad_out,
    value_weight,
    gate_weight,
    depth_taps,
    norm_gain,
    norm_shift,
    out_weight,
    lengths,
):
    R, NF, D = normed.shape
    K, CW = depth_taps.shape
    NS = lax.axis_size("seq")
    M = 8 * NS
    F = min(512, NF)
    TM = min(512, NF)
    TC = min(64, F)
    NCH = R * NF // F
    DP = D // NS
    cfg = (R, NF, D, NS, F, TM, TC)
    vmem = pl.BlockSpec(memory_space=pltpu.VMEM)
    hbm = pl.BlockSpec(memory_space=pl.ANY)
    dma = pltpu.SemaphoreType.DMA
    padded = NF + 2 * PAD
    out_shape = (
        jax.ShapeDtypeStruct((R, 8, NS * NF), BF16),
        jax.ShapeDtypeStruct((DP, CW), F32),
        jax.ShapeDtypeStruct((DP, CW), F32),
        jax.ShapeDtypeStruct((DP, CW), F32),
        jax.ShapeDtypeStruct((K, CW), F32),
        jax.ShapeDtypeStruct((1, CW), F32),
        jax.ShapeDtypeStruct((1, CW), F32),
    )
    scratch = [
        pltpu.VMEM((R, NF, D), BF16),
        pltpu.VMEM((R, NF, D), BF16),
        pltpu.VMEM((D, 2 * LANES), BF16),
        pltpu.VMEM((D, LANES), BF16),
        pltpu.VMEM((D, 2 * LANES), BF16),
        pltpu.VMEM((M, D), BF16),
        pltpu.VMEM((4, 2 * M, 2 * LANES), BF16),
        pltpu.VMEM((2, 2 * M, 2 * LANES), BF16),
        pltpu.VMEM((R, padded, LANES), F32),
        pltpu.VMEM((R, NF, LANES), F32),
        pltpu.VMEM((R, NF, LANES), F32),
        pltpu.VMEM((R, padded, LANES), F32),
        pltpu.VMEM((R, padded, LANES), F32),
        pltpu.VMEM((R, padded, LANES), F32),
        pltpu.VMEM((R, NF, LANES), BF16),
        pltpu.VMEM((2, 2, R, EDGE, LANES), F32),
        pltpu.VMEM((2, 2, R, EDGE, LANES), F32),
        pltpu.VMEM((NS, 8, LANES), F32),
        pltpu.VMEM((NS, 8, LANES), F32),
        pltpu.VMEM((NS, 16, LANES), F32),
        pltpu.VMEM((NCH, F, LANES), BF16),
        pltpu.VMEM((NCH, F, LANES), BF16),
        pltpu.VMEM((NCH, 2, F, 2 * LANES), BF16),
        pltpu.VMEM((NCH, 2, F, 2 * LANES), BF16),
        pltpu.VMEM((NCH, M, F), BF16),
        pltpu.VMEM((NCH, M, F), BF16),
        pltpu.VMEM((NCH, NS, 8, F), BF16),
        pltpu.VMEM((K, 8, LANES), F32),
        pltpu.VMEM((2 * LANES, D), F32),
        pltpu.VMEM((LANES, D), F32),
        pltpu.VMEM((3, D, LANES), F32),
        pltpu.VMEM((3, NS, DP, LANES), F32),
        dma((3 + 2 * R,)),
        dma((4,)),
        dma((4,)),
        dma((3,)),
        dma((3,)),
        dma((2,)),
        dma((2,)),
        dma,
        dma,
        dma((2 * NCH,)),
        dma((2 * NCH,)),
        dma((NCH,)),
        dma((NCH,)),
        dma((NCH,)),
        dma((NCH,)),
        dma((NCH,)),
        dma((NCH,)),
        dma((NCH,)),
        dma((3,)),
        dma((3,)),
    ]
    outs = pl.pallas_call(
        functools.partial(kernel, cfg),
        out_shape=tuple(pltpu.VMEM(o.shape, o.dtype) for o in out_shape),
        in_specs=[pl.BlockSpec(memory_space=pltpu.SMEM)] + [hbm] * 5 + [vmem] * 3,
        out_specs=(vmem,) * 7,
        scratch_shapes=scratch,
        compiler_params=pltpu.CompilerParams(
            collective_id=0, has_side_effects=True, vmem_limit_bytes=60 * 1024 * 1024
        ),
        cost_estimate=pl.CostEstimate(
            flops=8 * 2 * R * NF * D * CW, bytes_accessed=4 * R * NF * D, transcendentals=0
        ),
    )(
        lengths,
        normed,
        grad_out,
        value_weight,
        gate_weight,
        out_weight,
        depth_taps,
        norm_gain.reshape(1, CW),
        norm_shift.reshape(1, CW),
    )
    held = [pltpu.with_memory_space_constraint(o, pltpu.VMEM) for o in outs]
    moved = pl.pallas_call(
        hand_on,
        out_shape=out_shape,
        in_specs=[vmem] * len(out_shape),
        out_specs=(hbm,) * len(out_shape),
        scratch_shapes=[dma((len(out_shape),))],
    )(*held)
    grad_in, grad_wv, grad_wg, grad_wo, grad_taps, grad_gain, grad_shift = moved
    return (
        grad_in,
        grad_wv,
        grad_wg,
        grad_wo,
        grad_taps,
        grad_gain.reshape(CW),
        grad_shift.reshape(CW),
    )


def solution(mesh):
    placed = (
        P(None, "seq", None),
        P(None, "seq", None),
        P(None, "tp"),
        P(None, "tp"),
        P(None, "tp"),
        P("tp"),
        P("tp"),
        P(None, "tp"),
        P(),
    )
    return jax.shard_map(
        per_device,
        mesh=mesh,
        in_specs=placed,
        out_specs=(
            P(None, ("seq", "tp"), None),
            P("seq", "tp"),
            P("seq", "tp"),
            P("seq", "tp"),
            P(None, "tp"),
            P("tp"),
            P("tp"),
        ),
        check_vma=False,
    )
```

time: 89.9 us -> 68.6 us (0.76)
  Pallas kernels: 78.8 us -> 67.8 us
  local copies, waits for them, and re-layouts: 9.98 us -> 0 us
    pallas_call x1 -> x2, Pallas kernels: 78.8 us -> 67.8 us  [the longest x1 66.8 us: per_device(): pl.pallas_call(functools.partial(kernel, cfg), out_shape=tuple((pltpu.VME...]
    unnamed x7 -> x0, local copies, waits for them, and re-layouts: 9.98 us -> none
where the time goes in v2:
time: 68.6 us; the launch traced here: 68.5 us
  Pallas kernels  67.8 us (99%)
    pallas_call x1, Pallas kernels, per_device(): pl.pallas_call(functools.partial(kernel, cfg), out_shape=tuple((pltpu.VME...  66.8 us

profile of v2, /device:TPU:0, one launch (start us, length us, event | category | flops | bytes accessed | tf_op | source)
XLA Modules:
  0.0 68.5 jit_solution(7610583071200303674)
XLA Ops:
  0.6 66.8 %shard_map.144 = (bf16[4,8,16384]{2,1,0:T(8,128)(2,1)S(1)}, f32[64,128]{1,0:T(8,128)S(1)}, f32[64,128]{1,0:T(8,128)S(1)}, f32[64,128]{1,0:T(8,128)S(1)}, f32[9,1...) custom-call(s32[4]{0:T(128)} %lengths.1, bf16[4,1024,1024]{2,1,0:T(8,128)(2,1)} %normed_h.1, ...), custom_call_target="tpu_custom_call" | custom-call | flops 8589934592 | bytes 16777216 | tf_op jit(solution)/shard_map/pallas_call | solution.py:721
  67.4 1.1 %shard_map.145 = (bf16[4,8,16384]{2,1,0:T(8,128)(2,1)}, f32[64,128]{1,0:T(8,128)}, f32[64,128]{1,0:T(8,128)}, f32[64,128]{1,0:T(8,128)}, f32[9,128]{1,0:T(8,128)}, /*index=5*/f32[1,128]{1,0:T(1,128)}, f32[1,128]{1,0:T(1,128)}) custom-call(bf16[4,8,16384]{2,1,0:T(8,128)(2,1)S(1)} %get-tuple-element.21.refs_0_, f32[64,128]{1,0:T(8,128)S(1)} %get-tuple-element.22.refs_1_, ...), custom_call_target="tpu_custom_call" | custom-call | tf_op jit(solution)/shard_map/pallas_call | solution.py:745

commit v3 on v2

--- a/solution.py
+++ b/solution.py
@@ -57,9 +57,11 @@
     wcat,
     wo,
     w_next,
-    pick_own,
     wd,
     wd_send,
+    wd_oth,
+    feats,
+    own_part,
     gp,
     gs,
     a2,
@@ -118,9 +120,8 @@
     core = lax.rem(t, 2)
     other = x * 2 + (1 - core)
     step = 1 - 2 * lax.rem(x, 2)
-    x_far = lax.rem(x + XN - step, XN)
-    pair = (x + step) * 2 + core
-    far = x_far * 2 + core
+    x_pair = (x + step, lax.rem(x + XN - step, XN))
+    pair = tuple(xp * 2 + core for xp in x_pair)
     up = lax.rem(s + 1, NS)
     down = lax.rem(s + NS - 1, NS)
 
@@ -133,13 +134,13 @@
         return carry
 
     lax.fori_loop(1, NS, greet, 0)
-    for mate in (other, pair, far):
+    for mate in (other,) + pair:
         pl.semaphore_signal(barrier, inc=1, device_id=(s, mate), device_id_type=MESH)
 
     loads = [
         pltpu.make_async_copy(wv_h, wcat.at[:, 0:LANES], load_sem.at[0]),
         pltpu.make_async_copy(wg_h, wcat.at[:, LANES : 2 * LANES], load_sem.at[1]),
-        pltpu.make_async_copy(wo_h, wo, load_sem.at[2]),
+        pltpu.make_async_copy(wo_h, wo.at[:, 0:LANES], load_sem.at[2]),
     ]
     for load in loads:
         load.start()
@@ -163,23 +164,26 @@
         want = (row // 8) * 64 + xd * 16 + cd * 8 + row % 8
         return jnp.where(col == want, 1.0, 0.0).astype(BF16)
 
+    feature = lax.broadcasted_iota(jnp.int32, (D, LANES), 0)
+    place = lax.broadcasted_iota(jnp.int32, (D, LANES), 1)
+    want = (place // 8) * 64 + x * 16 + core * 8 + place % 8
+    wo[:, LANES : 2 * LANES] = jnp.where(
+        jnp.logical_and(feature == want, place < M), 1.0, 0.0
+    ).astype(BF16)
     loads[0].wait()
     loads[1].wait()
 
-    def pick_weights(source, group):
-        for side, xd in enumerate((x, x_far)):
-            rows = slice(side * M, (side + 1) * M)
-            wd[group, rows] = mm(picker(xd, core), source[...]).astype(BF16)
-            wd_send[group, rows] = mm(picker(xd, 1 - core), source[...]).astype(BF16)
-
-    def weight_swap(group):
-        return remote(
-            wd_send.at[group],
-            wd.at[2 + group],
-            wx_send.at[group],
-            wx_recv.at[group],
-            (s, other),
-        )
+    def pick_weights():
+        for cd, out in ((core, wd), (1 - core, wd_send)):
+            pick = picker(x, cd)
+            own = mm(pick, wcat[...]).astype(BF16)
+            for half in range(2):
+                out[half, 0, 0:M] = own
+                out[half, 1, 0:M] = mm(pick, w_next[half]).astype(BF16)
+            for half in range(2):
+                pick = picker(x_pair[1 - half], cd)
+                out[half, 0, M : 2 * M] = mm(pick, wcat[...]).astype(BF16)
+                out[half, 1, M : 2 * M] = mm(pick, w_next[half]).astype(BF16)
 
     tacc[...] = jnp.zeros_like(tacc)
     wacc[...] = jnp.zeros_like(wacc)
@@ -254,8 +258,13 @@
     lax.fori_loop(0, R * per_rec, forward, 0)
     pl.semaphore_wait(barrier, NS - 1 + 3)
     send_edges(0, gp)
-    next_weights = remote(wcat, w_next, wn_send, wn_recv, (s, pair))
-    next_weights.start()
+    next_weights = [
+        remote(wcat, w_next.at[half], wn_send.at[half], wn_recv.at[half], (s, pair[half]))
+        for half in range(2)
+    ]
+    for copy in next_weights:
+        copy.start()
+    weight_swap = remote(wd_send, wd_oth, wx_send, wx_recv, (s, other))
 
     tap_rows = [taps[k : k + 1, :] for k in range(K)]
     tiles = NF // TC
@@ -289,7 +298,9 @@
         def _():
             grads_load(r).wait()
 
-        gn[r, pl.ds(row0 + PAD, TM)] = mm(gv[r, pl.ds(row0, TM), :], wo[...])
+        both = mm(gv[r, pl.ds(row0, TM), :], wo[...])
+        gn[r, pl.ds(row0 + PAD, TM)] = both[:, :LANES]
+        feats[r, pl.ds(row0, TM)] = both[:, LANES:].astype(BF16)
         return carry
 
     lax.fori_loop(0, per_rec, back_one, 0)
@@ -345,9 +356,6 @@
         return r, pl.multiple_of(lax.rem(q, cpr) * F, F)
 
     lax.fori_loop(per_rec, R * per_rec, back_one, 0)
-    pick_weights(wcat, 0)
-    weight_swap(0).start()
-    pick_own[...] = picker(x, core)
 
     total = collect(red_a, 0)
     count = (lengths[0] + lengths[1] + lengths[2] + lengths[3]).astype(F32)
@@ -409,9 +417,10 @@
         wrecv[index, s] = wsend[index, pl.ds(pl.multiple_of(s * DP, DP), DP)]
 
     turn_weight(2, woacc, 0)
-    next_weights.wait_recv()
-    pick_weights(w_next, 1)
-    weight_swap(1).start()
+    for copy in next_weights:
+        copy.wait_recv()
+    pick_weights()
+    weight_swap.start()
     total = collect(red_b, 1)
     ship_weight(2)
     gshift[...] = total[0:1]
@@ -436,25 +445,25 @@
         lax.fori_loop(0, padded_rows // TE, conv_grad_tile, 0)
 
     def swap_copy(q, group):
-        index = 2 * q + group
         return remote(
             gmine.at[q, group],
             gother.at[q, group],
-            ge_send.at[index],
-            ge_recv.at[index],
+            ge_send,
+            ge_recv.at[2 * q + group],
             (s, other),
         )
 
-    def pair_copy(q):
-        return remote(gg_out.at[q], gg_in.at[q], gg_send.at[q], gg_recv.at[q], (s, pair))
-
-    def far_copy(q):
-        return remote(far_out.at[q], far_in.at[q], fr_send.at[q], fr_recv.at[q], (s, far))
-
-    def partial(q, side):
-        rows = slice(side * M, (side + 1) * M)
-        total = mm_t(wd[0, rows], gmine[q, 0]) + mm_t(wd[1, rows], gmine[q, 1])
-        return total + (mm_t(wd[2, rows], gother[q, 0]) + mm_t(wd[3, rows], gother[q, 1]))
+    def turn_of(i):
+        half = lax.rem(i, 2)
+        return half, half * (NCH // 2) + lax.div(i, 2)
+
+    def pair_copy(half, q):
+        to = pair[0] * (1 - half) + pair[1] * half
+        return remote(gg_out.at[q], gg_in.at[q], gg_send, gg_recv.at[q], (s, to))
+
+    def far_copy(half, q):
+        to = pair[1] * (1 - half) + pair[0] * half
+        return remote(far_out.at[q], far_in.at[q], fr_send, fr_recv.at[q], (s, to))
 
     def pointwise_grads(q):
         r, base = chunk_place(q)
@@ -480,22 +489,30 @@
         for k in range(K):
             tacc[k] = taps_sum[k]
 
-    def pair_grads(q):
+    def pair_grads(half, q):
         r, row0 = chunk_place(q)
-        both = mm(nv[r, pl.ds(row0, F), :], w_next[...])
+        both = mm(nv[r, pl.ds(row0, F), :], w_next[half])
         gate = jax.nn.sigmoid(both[:, LANES:])
         unit = both[:, :LANES] * gate
-        pair_copy(q).wait_recv()
+        pair_copy(half, q).wait_recv()
         grad = gg_in[q].astype(F32)
         gmine[q, 1, :, 0:LANES] = (grad * gate).astype(BF16)
         gmine[q, 1, :, LANES : 2 * LANES] = (grad * (unit * (1.0 - gate))).astype(BF16)
         swap_copy(q, 1).start()
 
-    def far_sends(q):
+    row = lax.broadcasted_iota(jnp.int32, (M, LANES), 0)
+    col = lax.broadcasted_iota(jnp.int32, (M, LANES), 1)
+    own_rows = jnp.where(row == col, 1.0, 0.0).astype(BF16)
+
+    def far_sends(half, q):
+        r, row0 = chunk_place(q)
+        total = mm_t(wd[half, 0], gmine[q, 0]) + mm_t(wd[half, 1], gmine[q, 1])
         for group in range(2):
             swap_copy(q, group).wait_recv()
-        far_out[q] = partial(q, 1).astype(BF16)
-        far_copy(q).start()
+        total = total + (mm_t(wd_oth[half, 0], gother[q, 0]) + mm_t(wd_oth[half, 1], gother[q, 1]))
+        far_out[q] = total[M:].astype(BF16)
+        far_copy(half, q).start()
+        own_part[q] = total[:M] + mm_t(own_rows, feats[r, pl.ds(row0, F)])
 
     def out_place(q, owner):
         r, row0 = chunk_place(q)
@@ -504,22 +521,18 @@
     def own_copy(q):
         return pltpu.make_async_copy(osend.at[q, s], out_place(q, s), aa_own.at[q])
 
-    def finish(q):
-        r, row0 = chunk_place(q)
-        total = partial(q, 0) + mm_t(pick_own[...], gv[r, pl.ds(row0, F), :])
-        far_copy(q).wait_recv()
-        total = total + far_in[q].astype(F32)
+    def finish(half, q):
+        far_copy(half, q).wait_recv()
+        total = own_part[q] + far_in[q].astype(F32)
         osend[q] = total.astype(BF16).reshape(NS, 8, F)
-        own_copy(q).start()
 
         def give(k, carry):
             p = lax.rem(s + k, NS)
-            remote(
-                osend.at[q, p], out_place(q, s), aa_send.at[q], aa_recv.at[q], (p, t)
-            ).start()
+            remote(osend.at[q, p], out_place(q, s), aa_send, aa_recv, (p, t)).start()
             return carry
 
         lax.fori_loop(1, NS, give, 0)
+        own_copy(q).start()
 
     def weight_part(q):
         r, row0 = chunk_place(q)
@@ -528,74 +541,61 @@
     for k in range(K, 16):
         red_c[s, k : k + 1] = jnp.zeros((1, LANES), F32)
 
-    LATE = NCH // 4
-
     def outward(i, carry):
-        @pl.when(lax.rem(i, cpr) == 0)
+        half, q = turn_of(i)
+
+        @pl.when(lax.rem(q, cpr) == 0)
         def _():
-            conv_grad(lax.div(i, cpr))
-
-        pointwise_grads(i)
-        pair_copy(i).start()
-        swap_copy(i, 0).start()
-
-        @pl.when(i < NCH - 2 * LATE)
-        def _():
-            weight_part(i)
-
+            conv_grad(lax.div(q, cpr))
+
+        pointwise_grads(q)
+        pair_copy(half, q).start()
+        swap_copy(q, 0).start()
+        weight_part(q)
         return carry
 
     lax.fori_loop(0, NCH, outward, 0)
-    for group in range(2):
-        weight_swap(group).wait_recv()
-
-    LAG_B, LAG_C = 1, 3
+    for index in range(2):
+        turn_weight(index, wacc, index * LANES)
+        ship_weight(index)
+    for k in range(K):
+        red_c[s, k : k + 1] = jnp.sum(tacc[k], axis=0, keepdims=True)
+    spread_from(red_c, 2)
+    weight_swap.wait_recv()
+    LAG_B, LAG_C = 1, 4
 
     def homeward(i, carry):
         @pl.when(i < NCH)
         def _():
-            pair_grads(i)
+            pair_grads(*turn_of(i))
+
+        @pl.when(i == NCH)
+        def _():
+            gtaps[...] = collect(red_c, 2)[0:K]
+
+            for index, out in ((2, gwo), (0, gwv), (1, gwg)):
+                slots = wrecv.at[index, pl.ds(0, NS - 1)]
+                pltpu.make_async_copy(slots, slots, wr_recv.at[index]).wait()
+                total = wrecv[index, 0]
+                for k in range(1, NS):
+                    total = total + wrecv[index, k]
+                out[...] = total
 
         @pl.when(jnp.logical_and(i >= LAG_B, i < NCH + LAG_B))
         def _():
-            far_sends(i - LAG_B)
-
-        @pl.when(i < LATE)
-        def _():
-            weight_part(NCH - 2 * LATE + 2 * i)
-            weight_part(NCH - 2 * LATE + 2 * i + 1)
-
-        @pl.when(i == LATE - 1)
-        def _():
-            for index in range(2):
-                turn_weight(index, wacc, index * LANES)
-                ship_weight(index)
-            for k in range(K):
-                red_c[s, k : k + 1] = jnp.sum(tacc[k], axis=0, keepdims=True)
-            spread_from(red_c, 2)
+            far_sends(*turn_of(i - LAG_B))
 
         @pl.when(i >= LAG_C)
         def _():
-            finish(i - LAG_C)
+            finish(*turn_of(i - LAG_C))
 
         return carry
 
     lax.fori_loop(0, NCH + LAG_C, homeward, 0)
 
-    gtaps[...] = collect(red_c, 2)[0:K]
-
-    for index, out in ((2, gwo), (0, gwv), (1, gwg)):
-        slots = wrecv.at[index, pl.ds(0, NS - 1)]
-        pltpu.make_async_copy(slots, slots, wr_recv.at[index]).wait()
-        total = wrecv[index, 0]
-        for k in range(1, NS):
-            total = total + wrecv[index, k]
-        out[...] = total
-
-    next_weights.wait_send()
-    for group in range(2):
-        weight_swap(group).wait_send()
-
+    for copy in next_weights:
+        copy.wait_send()
+    weight_swap.wait_send()
     for kind in range(2):
         for copy in edge_copies(kind):
             copy.wait_send()
@@ -606,18 +606,17 @@
         slots = wrecv.at[index, pl.ds(0, NS - 1)]
         pltpu.make_async_copy(slots, slots, wr_send.at[index]).wait()
 
-    def drain(q, carry):
-        for group in range(2):
-            swap_copy(q, group).wait_send()
-        pair_copy(q).wait_send()
-        far_copy(q).wait_send()
+    def sent(whole, semaphore):
+        pltpu.make_async_copy(whole, whole, semaphore).wait()
+
+    sent(gmine, ge_send)
+    sent(gg_out, gg_send)
+    sent(far_out, fr_send)
+    for q in range(NCH):
         own_copy(q).wait()
-        part = osend.at[q, pl.ds(0, NS - 1)]
-        pltpu.make_async_copy(part, part, aa_send.at[q]).wait()
-        pltpu.make_async_copy(part, part, aa_recv.at[q]).wait()
-        return carry
-
-    lax.fori_loop(0, NCH, drain, 0)
+    others = osend.at[:, pl.ds(0, NS - 1)]
+    sent(others, aa_send)
+    sent(others, aa_recv)
 
 
 def hand_on(*refs):
@@ -668,11 +667,13 @@
         pltpu.VMEM((R, NF, D), BF16),
         pltpu.VMEM((R, NF, D), BF16),
         pltpu.VMEM((D, 2 * LANES), BF16),
-        pltpu.VMEM((D, LANES), BF16),
         pltpu.VMEM((D, 2 * LANES), BF16),
-        pltpu.VMEM((M, D), BF16),
-        pltpu.VMEM((4, 2 * M, 2 * LANES), BF16),
-        pltpu.VMEM((2, 2 * M, 2 * LANES), BF16),
+        pltpu.VMEM((2, D, 2 * LANES), BF16),
+        pltpu.VMEM((2, 2, 2 * M, 2 * LANES), BF16),
+        pltpu.VMEM((2, 2, 2 * M, 2 * LANES), BF16),
+        pltpu.VMEM((2, 2, 2 * M, 2 * LANES), BF16),
+        pltpu.VMEM((R, NF, LANES), BF16),
+        pltpu.VMEM((NCH, M, F), F32),
         pltpu.VMEM((R, padded, LANES), F32),
         pltpu.VMEM((R, NF, LANES), F32),
         pltpu.VMEM((R, NF, LANES), F32),
@@ -702,18 +703,18 @@
         dma((4,)),
         dma((3,)),
         dma((3,)),
+        dma,
+        dma,
         dma((2,)),
         dma((2,)),
         dma,
+        dma((2 * NCH,)),
         dma,
-        dma((2 * NCH,)),
-        dma((2 * NCH,)),
         dma((NCH,)),
+        dma,
         dma((NCH,)),
-        dma((NCH,)),
-        dma((NCH,)),
-        dma((NCH,)),
-        dma((NCH,)),
+        dma,
+        dma,
         dma((NCH,)),
         dma((3,)),
         dma((3,)),

time: 68.6 us -> 63.9 us (0.931)
  Pallas kernels: 67.8 us -> 63.1 us
    pallas_call x1, Pallas kernels: 66.8 us -> 62 us  [per_device(): pl.pallas_call(functools.partial(kernel, cfg), out_shape=tuple((pltpu.VME...]
where the time goes in v3:
time: 63.9 us; the launch traced here: 63.7 us
  Pallas kernels  63.1 us (99%)
  between operations  0.64 us (1%)
    pallas_call x1, Pallas kernels, per_device(): pl.pallas_call(functools.partial(kernel, cfg), out_shape=tuple((pltpu.VME...  62 us

profile of v3, /device:TPU:0, one launch (start us, length us, event | category | flops | bytes accessed | tf_op | source)
XLA Modules:
  0.0 63.7 jit_solution(13799907880356793643)
XLA Ops:
  0.6 62.0 %shard_map.144 = (bf16[4,8,16384]{2,1,0:T(8,128)(2,1)S(1)}, f32[64,128]{1,0:T(8,128)S(1)}, f32[64,128]{1,0:T(8,128)S(1)}, f32[64,128]{1,0:T(8,128)S(1)}, f32[9,1...) custom-call(s32[4]{0:T(128)} %lengths.1, bf16[4,1024,1024]{2,1,0:T(8,128)(2,1)} %normed_h.1, ...), custom_call_target="tpu_custom_call" | custom-call | flops 8589934592 | bytes 16777216 | tf_op jit(solution)/shard_map/pallas_call | solution.py:722
  62.7 1.1 %shard_map.145 = (bf16[4,8,16384]{2,1,0:T(8,128)(2,1)}, f32[64,128]{1,0:T(8,128)}, f32[64,128]{1,0:T(8,128)}, f32[64,128]{1,0:T(8,128)}, f32[9,128]{1,0:T(8,128)}, /*index=5*/f32[1,128]{1,0:T(1,128)}, f32[1,128]{1,0:T(1,128)}) custom-call(bf16[4,8,16384]{2,1,0:T(8,128)(2,1)S(1)} %get-tuple-element.21.refs_0_, f32[64,128]{1,0:T(8,128)S(1)} %get-tuple-element.22.refs_1_, ...), custom_call_target="tpu_custom_call" | custom-call | tf_op jit(solution)/shard_map/pallas_call | solution.py:746

commit v4 on v3

--- a/solution.py
+++ b/solution.py
@@ -399,7 +399,7 @@
         for b in range(D // LANES):
             wsend[index, b * LANES : (b + 1) * LANES, :] = jnp.transpose(
                 acc[first : first + LANES, b * LANES : (b + 1) * LANES]
-            )
+            ).astype(BF16)
 
     def ship_weight(index):
         def give(k, carry):
@@ -551,16 +551,14 @@
         pointwise_grads(q)
         pair_copy(half, q).start()
         swap_copy(q, 0).start()
-        weight_part(q)
+
+        @pl.when(i < NCH - 8)
+        def _():
+            weight_part(q)
+
         return carry
 
     lax.fori_loop(0, NCH, outward, 0)
-    for index in range(2):
-        turn_weight(index, wacc, index * LANES)
-        ship_weight(index)
-    for k in range(K):
-        red_c[s, k : k + 1] = jnp.sum(tacc[k], axis=0, keepdims=True)
-    spread_from(red_c, 2)
     weight_swap.wait_recv()
     LAG_B, LAG_C = 1, 4
 
@@ -568,6 +566,20 @@
         @pl.when(i < NCH)
         def _():
             pair_grads(*turn_of(i))
+
+        @pl.when(i < 2)
+        def _():
+            for k in range(4):
+                weight_part(turn_of(NCH - 8 + 4 * i + k)[1])
+
+        @pl.when(i == 1)
+        def _():
+            for index in range(2):
+                turn_weight(index, wacc, index * LANES)
+                ship_weight(index)
+            for k in range(K):
+                red_c[s, k : k + 1] = jnp.sum(tacc[k], axis=0, keepdims=True)
+            spread_from(red_c, 2)
 
         @pl.when(i == NCH)
         def _():
@@ -576,9 +588,9 @@
             for index, out in ((2, gwo), (0, gwv), (1, gwg)):
                 slots = wrecv.at[index, pl.ds(0, NS - 1)]
                 pltpu.make_async_copy(slots, slots, wr_recv.at[index]).wait()
-                total = wrecv[index, 0]
+                total = wrecv[index, 0].astype(F32)
                 for k in range(1, NS):
-                    total = total + wrecv[index, k]
+                    total = total + wrecv[index, k].astype(F32)
                 out[...] = total
 
         @pl.when(jnp.logical_and(i >= LAG_B, i < NCH + LAG_B))
@@ -645,8 +657,8 @@
     NS = lax.axis_size("seq")
     M = 8 * NS
     F = min(512, NF)
-    TM = min(512, NF)
-    TC = min(64, F)
+    TM = min(1024, NF)
+    TC = min(128, F)
     NCH = R * NF // F
     DP = D // NS
     cfg = (R, NF, D, NS, F, TM, TC)
@@ -696,8 +708,8 @@
         pltpu.VMEM((K, 8, LANES), F32),
         pltpu.VMEM((2 * LANES, D), F32),
         pltpu.VMEM((LANES, D), F32),
-        pltpu.VMEM((3, D, LANES), F32),
-        pltpu.VMEM((3, NS, DP, LANES), F32),
+        pltpu.VMEM((3, D, LANES), BF16),
+        pltpu.VMEM((3, NS, DP, LANES), BF16),
         dma((3 + 2 * R,)),
         dma((4,)),
         dma((4,)),

time: 63.9 us -> 61.6 us (0.964)
  Pallas kernels: 63.1 us -> 60.8 us
    pallas_call x1, Pallas kernels: 62 us -> 59.7 us  [per_device(): pl.pallas_call(functools.partial(kernel, cfg), out_shape=tuple((pltpu.VME...]
where the time goes in v4:
time: 61.6 us; the launch traced here: 61.4 us
  Pallas kernels  60.8 us (99%)
  between operations  0.64 us (1%)
    pallas_call x1, Pallas kernels, per_device(): pl.pallas_call(functools.partial(kernel, cfg), out_shape=tuple((pltpu.VME...  59.7 us

profile of v4, /device:TPU:0, one launch (start us, length us, event | category | flops | bytes accessed | tf_op | source)
XLA Modules:
  0.0 61.4 jit_solution(15969747285628083031)
XLA Ops:
  0.6 59.7 %shard_map.144 = (bf16[4,8,16384]{2,1,0:T(8,128)(2,1)S(1)}, f32[64,128]{1,0:T(8,128)S(1)}, f32[64,128]{1,0:T(8,128)S(1)}, f32[64,128]{1,0:T(8,128)S(1)}, f32[9,1...) custom-call(s32[4]{0:T(128)} %lengths.1, bf16[4,1024,1024]{2,1,0:T(8,128)(2,1)} %normed_h.1, ...), custom_call_target="tpu_custom_call" | custom-call | flops 8589934592 | bytes 16777216 | tf_op jit(solution)/shard_map/pallas_call | solution.py:734
  60.3 1.1 %shard_map.145 = (bf16[4,8,16384]{2,1,0:T(8,128)(2,1)}, f32[64,128]{1,0:T(8,128)}, f32[64,128]{1,0:T(8,128)}, f32[64,128]{1,0:T(8,128)}, f32[9,128]{1,0:T(8,128)}, /*index=5*/f32[1,128]{1,0:T(1,128)}, f32[1,128]{1,0:T(1,128)}) custom-call(bf16[4,8,16384]{2,1,0:T(8,128)(2,1)S(1)} %get-tuple-element.21.refs_0_, f32[64,128]{1,0:T(8,128)S(1)} %get-tuple-element.22.refs_1_, ...), custom_call_target="tpu_custom_call" | custom-call | tf_op jit(solution)/shard_map/pallas_call | solution.py:758

commit v5 on v4

--- a/solution.py
+++ b/solution.py
@@ -173,17 +173,20 @@
     loads[0].wait()
     loads[1].wait()
 
-    def pick_weights():
+    def pick_weights(first):
         for cd, out in ((core, wd), (1 - core, wd_send)):
             pick = picker(x, cd)
-            own = mm(pick, wcat[...]).astype(BF16)
+            if first:
+                own = mm(pick, wcat[...]).astype(BF16)
             for half in range(2):
-                out[half, 0, 0:M] = own
-                out[half, 1, 0:M] = mm(pick, w_next[half]).astype(BF16)
+                if first:
+                    out[half, 0, 0:M] = own
+                else:
+                    out[half, 1, 0:M] = mm(pick, w_next[half]).astype(BF16)
             for half in range(2):
                 pick = picker(x_pair[1 - half], cd)
-                out[half, 0, M : 2 * M] = mm(pick, wcat[...]).astype(BF16)
-                out[half, 1, M : 2 * M] = mm(pick, w_next[half]).astype(BF16)
+                source = wcat[...] if first else w_next[half]
+                out[half, 0 if first else 1, M : 2 * M] = mm(pick, source).astype(BF16)
 
     tacc[...] = jnp.zeros_like(tacc)
     wacc[...] = jnp.zeros_like(wacc)
@@ -356,6 +359,7 @@
         return r, pl.multiple_of(lax.rem(q, cpr) * F, F)
 
     lax.fori_loop(per_rec, R * per_rec, back_one, 0)
+    pick_weights(True)
 
     total = collect(red_a, 0)
     count = (lengths[0] + lengths[1] + lengths[2] + lengths[3]).astype(F32)
@@ -419,7 +423,7 @@
     turn_weight(2, woacc, 0)
     for copy in next_weights:
         copy.wait_recv()
-    pick_weights()
+    pick_weights(False)
     weight_swap.start()
     total = collect(red_b, 1)
     ship_weight(2)
@@ -560,7 +564,7 @@
 
     lax.fori_loop(0, NCH, outward, 0)
     weight_swap.wait_recv()
-    LAG_B, LAG_C = 1, 4
+    LAG_B, LAG_C = 1, 5
 
     def homeward(i, carry):
         @pl.when(i < NCH)

time: 61.6 us -> 60.3 us (0.979)
  Pallas kernels: 60.8 us -> 59.5 us
    pallas_call x1, Pallas kernels: 59.7 us -> 58.5 us  [per_device(): pl.pallas_call(functools.partial(kernel, cfg), out_shape=tuple((pltpu.VME...]
where the time goes in v5:
time: 60.3 us; the launch traced here: 60.2 us
  Pallas kernels  59.5 us (99%)
  between operations  0.64 us (1%)
    pallas_call x1, Pallas kernels, per_device(): pl.pallas_call(functools.partial(kernel, cfg), out_shape=tuple((pltpu.VME...  58.5 us

profile of v5, /device:TPU:0, one launch (start us, length us, event | category | flops | bytes accessed | tf_op | source)
XLA Modules:
  0.0 60.2 jit_solution(7091073237608631739)
XLA Ops:
  0.6 58.5 %shard_map.144 = (bf16[4,8,16384]{2,1,0:T(8,128)(2,1)S(1)}, f32[64,128]{1,0:T(8,128)S(1)}, f32[64,128]{1,0:T(8,128)S(1)}, f32[64,128]{1,0:T(8,128)S(1)}, f32[9,1...) custom-call(s32[4]{0:T(128)} %lengths.1, bf16[4,1024,1024]{2,1,0:T(8,128)(2,1)} %normed_h.1, ...), custom_call_target="tpu_custom_call" | custom-call | flops 8589934592 | bytes 16777216 | tf_op jit(solution)/shard_map/pallas_call | solution.py:738
  59.1 1.1 %shard_map.145 = (bf16[4,8,16384]{2,1,0:T(8,128)(2,1)}, f32[64,128]{1,0:T(8,128)}, f32[64,128]{1,0:T(8,128)}, f32[64,128]{1,0:T(8,128)}, f32[9,128]{1,0:T(8,128)}, /*index=5*/f32[1,128]{1,0:T(1,128)}, f32[1,128]{1,0:T(1,128)}) custom-call(bf16[4,8,16384]{2,1,0:T(8,128)(2,1)S(1)} %get-tuple-element.21.refs_0_, f32[64,128]{1,0:T(8,128)S(1)} %get-tuple-element.22.refs_1_, ...), custom_call_target="tpu_custom_call" | custom-call | tf_op jit(solution)/shard_map/pallas_call | solution.py:762
